TPU v7x, 1024 devices: a whole 8x8x8 slice. The times are simulated.
1024 devices in a mesh: far: 16 (over z, y_lo), near: 64 (over x, y_hi, core).
Axes of the slice: x: 8, y: 8 (y_hi: 4, y_lo: 2; y = y_hi * 2 + y_lo), z: 8, core: 2. Of those that a mesh axis runs over, the one named last changes fastest.
Arguments:
- state_real: float32 [16, 64, 2, 128, 128], P('far', 'near'), may hold values from -5 to 5
- state_imag: float32 [16, 64, 2, 128, 128], P('far', 'near'), may hold values from -5 to 5
- gate_real: float32 [2, 4, 3, 128, 128], replicated, may hold values from -0.375 to 0.375
- gate_imag: float32 [2, 4, 3, 128, 128], replicated, may hold values from -0.375 to 0.375
Outputs:
- final_real: float32 [16, 64, 2, 128, 128], P('far', 'near')
- final_imag: float32 [16, 64, 2, 128, 128], P('far', 'near')
All inputs are finite; a program needn't handle non-finite values.
Results may differ from a plain program's by a relative error of at most 0.000071.
Values sent between devices are 32-bit elements; how exact they have to be, the bound alone decides.
No kernel may reach another device: no remote copies, remote signals or barrier semaphores. Data moves between devices by JAX's collectives and lax.ppermute only.
A program may use at most 32 MiB of HBM per device.

v0:
```python
import jax
import jax.numpy as jnp
from jax import lax
from jax.sharding import PartitionSpec as P


def side_by_side(arrays, axis, split_dim, concat_dim, along):
    ends, at = ([], 0)
    for a in arrays[:-1]:
        at += a.shape[along]
        ends.append(at)
    both = jnp.concatenate(arrays, axis=along)
    return tuple(
        jnp.split(
            lax.all_to_all(both, axis, split_axis=split_dim, concat_axis=concat_dim, tiled=True),
            ends,
            axis=along,
        )
    )


def gate_low(x, g):
    return jnp.einsum(
        "...l,jl->...j", x, g, precision=lax.Precision.HIGHEST, preferred_element_type=jnp.float32
    )


def gate_mid(x, g):
    return jnp.einsum(
        "...ml,jm->...jl", x, g, precision=lax.Precision.HIGHEST, preferred_element_type=jnp.float32
    )


def gate_top(x, g):
    high, width, lows = (x.shape[-3], x.shape[-2], x.shape[-1])
    upper = g.shape[0] // high
    lead = x.shape[:-3]
    viewed = x.reshape(lead + (high, upper, width // upper, lows))
    matrix = g.reshape((g.shape[0], high, upper))
    out = jnp.einsum(
        "...hkrl,jhk->...jrl",
        viewed,
        matrix,
        precision=lax.Precision.HIGHEST,
        preferred_element_type=jnp.float32,
    )
    return out.reshape(lead + (high, width, lows))


def complex_gate(form, real, imag, greal, gimag):
    new_real = form(real, greal) - form(imag, gimag)
    new_imag = form(imag, greal) + form(real, gimag)
    return (new_real, new_imag)


def merged_rows(x):
    return x.reshape((1, 1, x.shape[2] * x.shape[3], x.shape[4]))


def on_device(state_real, state_imag, gate_real, gate_imag):
    real, imag = (state_real, state_imag)
    forms = (gate_low, gate_mid, gate_top)
    shape = state_real.shape
    for rnd in range(gate_real.shape[0]):
        for section in range(4):
            if section == 2:
                order = [1, 0, 2]
            else:
                order = [0, 1, 2]
            early = []
            later = order[len(early) :]
            pair = (real, imag)
            if section == 0:
                moved = side_by_side((merged_rows(pair[0]), merged_rows(pair[1])), "far", 2, 2, 0)
                pair = (moved[0].reshape(shape), moved[1].reshape(shape))
            elif section == 1:
                pair = side_by_side((pair[0], pair[1]), "near", 3, 3, 0)
            elif section == 2:
                pair = side_by_side((pair[0], pair[1]), "near", 4, 4, 0)
            else:
                moved = side_by_side((merged_rows(pair[0]), merged_rows(pair[1])), "near", 2, 2, 0)
                pair = (moved[0].reshape(shape), moved[1].reshape(shape))
            for which in later:
                pair = complex_gate(
                    forms[which],
                    pair[0],
                    pair[1],
                    gate_real[rnd, section, which],
                    gate_imag[rnd, section, which],
                )
            real, imag = pair
    return (real, imag)


def solution(mesh):
    return jax.shard_map(
        on_device,
        mesh=mesh,
        in_specs=(P("far", "near", None, None, None), P("far", "near", None, None, None), P(), P()),
        out_specs=(P("far", "near", None, None, None), P("far", "near", None, None, None)),
        check_vma=False,
    )
```

profile of v0, /device:TPU:1, one launch (start us, length us, event | category | flops | bytes accessed | tf_op | source)
XLA Modules:
  0.0 217.0 jit_solution(6805037588123794739)
XLA Ops:
  0.6 2.0 pad_maximum_fusion
  2.7 18.5 %all-to-all-start = ((f32[2,1,256,128]{3,1,0,2:T(1,128)}), f32[2,1,256,128]{3,1,0,2:T(1,128)S(1)}, u32[]{:S(2)}, u32[]{:S(2)}) async-start(f32[2,1,256,128]{3,1,0,2:T(1,128)} %pad_maximum_fusion), calls=%async_computation | async-start | bytes 524288 | tf_op jit(solution)/shard_map/all_to_all | solution.py:15
  21.2 1.9 fusion.229
  24.9 5.1 %all-to-all-done = f32[2,1,256,128]{3,1,0,2:T(1,128)S(1)} async-done(((f32[2,1,256,128]{3,1,0,2:T(1,128)}), f32[2,1,256,128]{3,1,0,2:T(1,128)S(1)}, u32[]{:S(2)}, u32[]{:S(2)}) %all-to-all-start) | async-done | bytes 262176 | tf_op jit(solution)/shard_map/all_to_all | solution.py:15
  35.0 15.7 %all-to-all-start.1 = ((f32[2,1,2,128,128]{4,2,1,0,3:T(2,128)}), f32[2,1,2,128,128]{4,2,1,0,3:T(2,128)S(1)}, u32[]{:S(2)}, u32[]{:S(2)}) async-start(f32[2,1,2,128,128]{4,2,1,0,3:T(2,128)} %copy.146), calls=%async_computation.1 | async-start | bytes 524288 | tf_op jit(solution)/shard_map/all_to_all | solution.py:15
  50.8 0.9 copy.151
  51.7 14.5 %all-to-all-done.1 = f32[2,1,2,128,128]{4,2,1,0,3:T(2,128)S(1)} async-done(((f32[2,1,2,128,128]{4,2,1,0,3:T(2,128)}), f32[2,1,2,128,128]{4,2,1,0,3:T(2,128)S(1)}, u32[]{:S(2)}, u32[]{:S(2)}) %all-to-all-start.1) | async-done | bytes 262176 | tf_op jit(solution)/shard_map/all_to_all | solution.py:15
  71.0 4.4 %all-to-all-start.2 = ((f32[2,1,2,128,128]{3,2,1,0,4:T(2,128)}), f32[2,1,2,128,128]{3,2,1,0,4:T(2,128)S(1)}, u32[]{:S(2)}, u32[]{:S(2)}) async-start(f32[2,1,2,128,128]{3,2,1,0,4:T(2,128)} %copy.157), calls=%async_computation.2 | async-start | bytes 524288 | tf_op jit(solution)/shard_map/all_to_all | solution.py:15
  75.4 0.9 copy.162
  76.3 0.9 copy.166
  77.2 13.7 %all-to-all-done.2 = f32[2,1,2,128,128]{3,2,1,0,4:T(2,128)S(1)} async-done(((f32[2,1,2,128,128]{3,2,1,0,4:T(2,128)}), f32[2,1,2,128,128]{3,2,1,0,4:T(2,128)S(1)}, u32[]{:S(2)}, u32[]{:S(2)}) %all-to-all-start.2) | async-done | bytes 262176 | tf_op jit(solution)/shard_map/all_to_all | solution.py:15
  95.3 1.0 copy.172
  96.3 4.3 %all-to-all-start.3 = ((f32[2,1,256,128]{3,1,0,2:T(1,128)}), f32[2,1,256,128]{3,1,0,2:T(1,128)S(1)}, u32[]{:S(2)}, u32[]{:S(2)}) async-start(f32[2,1,256,128]{3,1,0,2:T(1,128)} %copy.172), calls=%async_computation.3 | async-start | bytes 524288 | tf_op jit(solution)/shard_map/all_to_all | solution.py:15
  100.6 0.9 copy.173
  101.6 0.9 copy.175
  102.5 13.8 %all-to-all-done.3 = f32[2,1,256,128]{3,1,0,2:T(1,128)S(1)} async-done(((f32[2,1,256,128]{3,1,0,2:T(1,128)}), f32[2,1,256,128]{3,1,0,2:T(1,128)S(1)}, u32[]{:S(2)}, u32[]{:S(2)}) %all-to-all-start.3) | async-done | bytes 262176 | tf_op jit(solution)/shard_map/all_to_all | solution.py:15
  120.3 1.0 copy.181
  121.2 3.5 %all-to-all-start.4 = ((f32[2,1,256,128]{3,1,0,2:T(1,128)}), f32[2,1,256,128]{3,1,0,2:T(1,128)S(1)}, u32[]{:S(2)}, u32[]{:S(2)}) async-start(f32[2,1,256,128]{3,1,0,2:T(1,128)} %copy.181), calls=%async_computation.4 | async-start | bytes 524288 | tf_op jit(solution)/shard_map/all_to_all | solution.py:15
  125.7 0.9 copy.184
  126.7 8.4 %all-to-all-done.4 = f32[2,1,256,128]{3,1,0,2:T(1,128)S(1)} async-done(((f32[2,1,256,128]{3,1,0,2:T(1,128)}), f32[2,1,256,128]{3,1,0,2:T(1,128)S(1)}, u32[]{:S(2)}, u32[]{:S(2)}) %all-to-all-start.4) | async-done | bytes 262176 | tf_op jit(solution)/shard_map/all_to_all | solution.py:15
  140.0 6.1 %all-to-all-start.5 = ((f32[2,1,2,128,128]{4,2,1,0,3:T(2,128)}), f32[2,1,2,128,128]{4,2,1,0,3:T(2,128)S(1)}, u32[]{:S(2)}, u32[]{:S(2)}) async-start(f32[2,1,2,128,128]{4,2,1,0,3:T(2,128)} %copy.190), calls=%async_computation.5 | async-start | bytes 524288 | tf_op jit(solution)/shard_map/all_to_all | solution.py:15
  146.1 0.9 copy.193
  147.0 0.9 copy.195
  148.0 13.8 %all-to-all-done.5 = f32[2,1,2,128,128]{4,2,1,0,3:T(2,128)S(1)} async-done(((f32[2,1,2,128,128]{4,2,1,0,3:T(2,128)}), f32[2,1,2,128,128]{4,2,1,0,3:T(2,128)S(1)}, u32[]{:S(2)}, u32[]{:S(2)}) %all-to-all-start.5) | async-done | bytes 262176 | tf_op jit(solution)/shard_map/all_to_all | solution.py:15
  166.5 4.3 %all-to-all-start.6 = ((f32[2,1,2,128,128]{3,2,1,0,4:T(2,128)}), f32[2,1,2,128,128]{3,2,1,0,4:T(2,128)S(1)}, u32[]{:S(2)}, u32[]{:S(2)}) async-start(f32[2,1,2,128,128]{3,2,1,0,4:T(2,128)} %copy.201), calls=%async_computation.6 | async-start | bytes 524288 | tf_op jit(solution)/shard_map/all_to_all | solution.py:15
  170.8 0.9 copy.206
  171.7 0.9 copy.210
  172.7 13.8 %all-to-all-done.6 = f32[2,1,2,128,128]{3,2,1,0,4:T(2,128)S(1)} async-done(((f32[2,1,2,128,128]{3,2,1,0,4:T(2,128)}), f32[2,1,2,128,128]{3,2,1,0,4:T(2,128)S(1)}, u32[]{:S(2)}, u32[]{:S(2)}) %all-to-all-start.6) | async-done | bytes 262176 | tf_op jit(solution)/shard_map/all_to_all | solution.py:15
  190.8 1.0 copy.216
  191.8 4.4 %all-to-all-start.7 = ((f32[2,1,256,128]{3,1,0,2:T(1,128)}), f32[2,1,256,128]{3,1,0,2:T(1,128)S(1)}, u32[]{:S(2)}, u32[]{:S(2)}) async-start(f32[2,1,256,128]{3,1,0,2:T(1,128)} %copy.216), calls=%async_computation.7 | async-start | bytes 524288 | tf_op jit(solution)/shard_map/all_to_all | solution.py:15
  197.2 0.9 copy.219
  198.1 13.7 %all-to-all-done.7 = f32[2,1,256,128]{3,1,0,2:T(1,128)S(1)} async-done(((f32[2,1,256,128]{3,1,0,2:T(1,128)}), f32[2,1,256,128]{3,1,0,2:T(1,128)S(1)}, u32[]{:S(2)}, u32[]{:S(2)}) %all-to-all-start.7) | async-done | bytes 262176 | tf_op jit(solution)/shard_map/all_to_all | solution.py:15
  (143 shorter events, 40.1 us)
Async XLA Ops:
  0.6 22.6 %copy-start.1 = (f32[2,4,3,128,128]{4,3,2,1,0:T(8,128)S(1)}, f32[2,4,3,128,128]{4,3,2,1,0:T(8,128)}, u32[]{:S(2)}) copy-start(f32[2,4,3,128,128]{4,3,2,1,0:T(8,128)} %param.7) | copy-start | bytes 4718596
  2.7 27.4 %all-to-all-start = ((f32[2,1,256,128]{3,1,0,2:T(1,128)}), f32[2,1,256,128]{3,1,0,2:T(1,128)S(1)}, u32[]{:S(2)}, u32[]{:S(2)}) async-start(f32[2,1,256,128]{3,1,0,2:T(1,128)} %pad_maximum_fusion), calls=%async_computation | async-start | bytes 524288 | tf_op jit(solution)/shard_map/all_to_all | solution.py:15
  21.1 9.1 %copy-start = (f32[2,4,3,128,128]{4,3,2,1,0:T(8,128)S(1)}, f32[2,4,3,128,128]{4,3,2,1,0:T(8,128)}, u32[]{:S(2)}) copy-start(f32[2,4,3,128,128]{4,3,2,1,0:T(8,128)} %param.6) | copy-start | bytes 4718596
  33.2 17.5 %copy-start.2 = (f32[1,1,1,128,128]{4,3,2,1,0:T(8,128)S(1)}, f32[1,1,1,128,128]{4,3,2,1,0:T(8,128)}, u32[]{:S(2)}) copy-start(f32[1,1,1,128,128]{4,3,2,1,0:T(8,128)} %get-tuple-element.16) | copy-start | bytes 196612
  35.0 31.2 %all-to-all-start.1 = ((f32[2,1,2,128,128]{4,2,1,0,3:T(2,128)}), f32[2,1,2,128,128]{4,2,1,0,3:T(2,128)S(1)}, u32[]{:S(2)}, u32[]{:S(2)}) async-start(f32[2,1,2,128,128]{4,2,1,0,3:T(2,128)} %copy.146), calls=%async_computation.1 | async-start | bytes 524288 | tf_op jit(solution)/shard_map/all_to_all | solution.py:15
  71.0 20.0 %all-to-all-start.2 = ((f32[2,1,2,128,128]{3,2,1,0,4:T(2,128)}), f32[2,1,2,128,128]{3,2,1,0,4:T(2,128)S(1)}, u32[]{:S(2)}, u32[]{:S(2)}) async-start(f32[2,1,2,128,128]{3,2,1,0,4:T(2,128)} %copy.157), calls=%async_computation.2 | async-start | bytes 524288 | tf_op jit(solution)/shard_map/all_to_all | solution.py:15
  96.3 20.0 %all-to-all-start.3 = ((f32[2,1,256,128]{3,1,0,2:T(1,128)}), f32[2,1,256,128]{3,1,0,2:T(1,128)S(1)}, u32[]{:S(2)}, u32[]{:S(2)}) async-start(f32[2,1,256,128]{3,1,0,2:T(1,128)} %copy.172), calls=%async_computation.3 | async-start | bytes 524288 | tf_op jit(solution)/shard_map/all_to_all | solution.py:15
  121.2 13.8 %all-to-all-start.4 = ((f32[2,1,256,128]{3,1,0,2:T(1,128)}), f32[2,1,256,128]{3,1,0,2:T(1,128)S(1)}, u32[]{:S(2)}, u32[]{:S(2)}) async-start(f32[2,1,256,128]{3,1,0,2:T(1,128)} %copy.181), calls=%async_computation.4 | async-start | bytes 524288 | tf_op jit(solution)/shard_map/all_to_all | solution.py:15
  140.0 21.7 %all-to-all-start.5 = ((f32[2,1,2,128,128]{4,2,1,0,3:T(2,128)}), f32[2,1,2,128,128]{4,2,1,0,3:T(2,128)S(1)}, u32[]{:S(2)}, u32[]{:S(2)}) async-start(f32[2,1,2,128,128]{4,2,1,0,3:T(2,128)} %copy.190), calls=%async_computation.5 | async-start | bytes 524288 | tf_op jit(solution)/shard_map/all_to_all | solution.py:15
  166.5 20.0 %all-to-all-start.6 = ((f32[2,1,2,128,128]{3,2,1,0,4:T(2,128)}), f32[2,1,2,128,128]{3,2,1,0,4:T(2,128)S(1)}, u32[]{:S(2)}, u32[]{:S(2)}) async-start(f32[2,1,2,128,128]{3,2,1,0,4:T(2,128)} %copy.201), calls=%async_computation.6 | async-start | bytes 524288 | tf_op jit(solution)/shard_map/all_to_all | solution.py:15
  191.8 20.0 %all-to-all-start.7 = ((f32[2,1,256,128]{3,1,0,2:T(1,128)}), f32[2,1,256,128]{3,1,0,2:T(1,128)S(1)}, u32[]{:S(2)}, u32[]{:S(2)}) async-start(f32[2,1,256,128]{3,1,0,2:T(1,128)} %copy.216), calls=%async_computation.7 | async-start | bytes 524288 | tf_op jit(solution)/shard_map/all_to_all | solution.py:15
where the time goes:
time: 218 us; the launch traced here: 217 us
  waiting for transfers between devices  96.8 us (44%)
  starting transfers between devices  61.2 us (28%)
  matrix products  28.6 us (13%)
  local copies, waits for them, and re-layouts  26.5 us (12%)
    all_to_all x8, waiting for transfers between devices, side_by_side(): lax.all_to_all(both, axis, split_axis=split_dim, concat_axis=concat_dim,...  96.8 us
    all_to_all x8, starting transfers between devices, side_by_side(): lax.all_to_all(both, axis, split_axis=split_dim, concat_axis=concat_dim,...  61.2 us
    dot_general x32, matrix products, gate_top(): jnp.einsum('...hkrl,jhk->...jrl', viewed, matrix, precision=lax.Precision...  10.1 us
    dot_general x32, matrix products, gate_low(): jnp.einsum('...l,jl->...j', x, g, precision=lax.Precision.HIGHEST, prefer...  9.78 us
    dot_general x32, matrix products, gate_mid(): jnp.einsum('...ml,jm->...jl', x, g, precision=lax.Precision.HIGHEST, pref...  8.7 us
    slice x9, local copies, waits for them, and re-layouts, on_device(): gate_imag[rnd, section, which]  8.26 us
    slice x9, local copies, waits for them, and re-layouts, on_device(): gate_real[rnd, section, which]  7.68 us
    concatenate x7, local copies, waits for them, and re-layouts, side_by_side(): both = jnp.concatenate(arrays, axis=along)  6.49 us
  transfers between devices with their start and end apart: 8, of which 8 were waited for; matrix products, arithmetic and copies ran while one was open for 7% of the time, Pallas kernels for 0%

commit v1 on v0

v1 whole, which is shorter than its diff:
```python
import functools

import jax
import jax.numpy as jnp
from jax import lax
from jax.experimental import pallas as pl
from jax.experimental.pallas import tpu as pltpu
from jax.sharding import PartitionSpec as P

F32, BF16 = jnp.float32, jnp.bfloat16
NN = (((1,), (0,)), ((), ()))
NT = (((1,), (1,)), ((), ()))


def split(x):
    hi = x.astype(BF16)
    return hi, (x - hi.astype(F32)).astype(BF16)


def mm(a, b, dims=NN):
    dot = functools.partial(lax.dot_general, dimension_numbers=dims, preferred_element_type=F32)
    return dot(a[0], b[0]) + (dot(a[0], b[1]) + dot(a[1], b[0]))


def cat(parts, axis):
    return jnp.concatenate(parts, axis)


def rows_of(x, n, count):
    return x[n * count : (n + 1) * count]


def merged(r, n):
    k = r.shape[1] // 2
    return r[:n, :k] - r[n:, k:], r[n:, :k] + r[:n, k:]


def big(real, imag):
    return cat([cat([real, -imag], 1), cat([imag, real], 1)], 0)


def lane_bit(shape, stride):
    return (lax.broadcasted_iota(jnp.int32, shape, 1) // stride) % 2 == 0


def swap(a, b, stride):
    even, lanes = lane_bit(a.shape, stride), a.shape[1]
    return (
        jnp.where(even, a, pltpu.roll(b, stride, 1)),
        jnp.where(even, pltpu.roll(a, lanes - stride, 1), b),
    )


def selector(bit):
    i = lax.broadcasted_iota(jnp.int32, (128, 128), 0)
    j = lax.broadcasted_iota(jnp.int32, (128, 128), 1)
    low, top = i % (1 << bit), i // 64
    mid = (i % 64) // (1 << bit)
    return jnp.where(j == mid * (2 << bit) + top * (1 << bit) + low, 1.0, 0.0).astype(BF16)


def columns_moved(x, sel):
    dot = functools.partial(lax.dot_general, dimension_numbers=NT, preferred_element_type=F32)
    hi, lo = split(x)
    return dot(hi, sel) + dot(lo, sel)


def gate(ref, at):
    return ref[pl.ds(at * 128, 128), :]


def odd_even(ref, at):
    return cat([ref[pl.ds(at * 128 + t, 64, 2), :] for t in range(2)], 0)


def rows_gate(gr, gi, s, sel, top_moved=False):
    mid, top = 3 * s + 1, 3 * s + 2
    m = columns_moved(cat([odd_even(gr, mid), odd_even(gi, mid)], 0), sel)
    if top_moved:
        c = split(cat([odd_even(gr, top), odd_even(gi, top)], 0))
    else:
        c = split(cat([gate(gr, top), gate(gi, top)], 0))
    left = lane_bit((64, 128), 64)
    real, imag = [], []
    for t in range(2):
        row_real, row_imag = [], []
        for u in range(2):
            diagonal = []
            for part in range(2):
                x = rows_of(m, part * 2 + t, 64)
                y = pltpu.roll(x, 64, 1)
                up, down = (x, y) if u == 0 else (y, x)
                diagonal.append(cat([jnp.where(left, up, 0.0), jnp.where(left, 0.0, down)], 0))
            r = mm(c, split(cat(diagonal, 1)))
            wr, wi = merged(r, 128)
            row_real.append(wr)
            row_imag.append(wi)
        real.append(cat(row_real, 1))
        imag.append(cat(row_imag, 1))
    return cat(real, 0), cat(imag, 0)


def product(a, b):
    n = a[0].shape[0]
    r = mm(split(cat(a, 0)), split(cat(b, 1)))
    return merged(r, n)


def low(gr, gi, s):
    return gate(gr, 3 * s), gate(gi, 3 * s)


def put(refs, x):
    refs[0][...], refs[1][...] = split(x)


def prepare_first(gr, gi, w0h, w0l, l25h, l25l):
    sel = selector(0)
    put((w0h, w0l), cat(rows_gate(gr, gi, 0, sel), 0))
    first = tuple(columns_moved(a, sel) for a in low(gr, gi, 2))
    x = product(low(gr, gi, 3), first)
    y = product((odd_even(gr, 15), odd_even(gi, 15)), low(gr, gi, 4))
    put((l25h, l25l), big(*product(y, x)))


def prepare_second(gr, gi, w12h, w12l, w3h, w3l):
    sel = selector(0)
    w = product(rows_gate(gr, gi, 2, sel, True), rows_gate(gr, gi, 1, sel))
    put((w12h, w12l), cat(w, 0))
    put((w3h, w3l), cat(rows_gate(gr, gi, 3, selector(1)), 0))


def prepare_third(gr, gi, w4h, w4l, w56h, w56l, l67h, l67l):
    sel = selector(0)
    put((w4h, w4l), cat(rows_gate(gr, gi, 4, sel), 0))
    w = product(rows_gate(gr, gi, 6, sel, True), rows_gate(gr, gi, 5, sel))
    put((w56h, w56l), cat(w, 0))
    first = tuple(columns_moved(a, sel) for a in low(gr, gi, 6))
    put((l67h, l67l), big(*product(low(gr, gi, 7), first)))


def prepare_fourth(gr, gi, w7h, w7l):
    sel = selector(0)
    w = cat(rows_gate(gr, gi, 7, sel), 0)
    put((w7h, w7l), cat([columns_moved(w[:, :128], sel), columns_moved(w[:, 128:], sel)], 1))


def read_blocks(ref):
    return cat(
        [cat([ref[:, p, t].reshape(128, 128) for t in range(2)], 0) for p in range(2)], 1
    )


def read_strided(ref):
    return cat(
        [cat([ref[pl.ds(p * 4 + o, 64, 8), :] for o in range(4)], 0) for p in range(2)], 1
    )


def phase0(sr, si, g0r, g0i, g1r, g1i, out):
    x = cat([cat([ref[pl.ds(t, 128, 2), :] for t in range(2)], 0) for ref in (sr, si)], 1)
    x = mm(split(x), split(big(g0r[...], g0i[...])), NT)
    x = mm(split(x), split(big(g1r[...], g1i[...])), NT)
    for p in range(2):
        for t in range(2):
            out[:, p, t] = x[t * 128 : (t + 1) * 128, p * 128 : (p + 1) * 128].reshape(16, 8, 128)


def phase1(x, w0h, w0l, l25h, l25l, out):
    o = merged(mm((w0h[...], w0l[...]), split(read_blocks(x))), 256)
    u = [swap(o[p][:128], o[p][128:], 1) for p in range(2)]
    rows = [u[p][v] for p in range(2) for v in range(2)]
    u = cat([cat([rows_of(r, f, 64) for r in rows], 0) for f in range(2)], 1)
    v = mm((l25h[...], l25l[...]), split(u))
    for p in range(2):
        for f in range(2):
            block = v[p * 128 : (p + 1) * 128, f * 128 : (f + 1) * 128]
            for t, y in enumerate(swap(block[:64], block[64:], 1)):
                out[pl.ds(p * 4 + t * 2 + f, 64, 8), :] = y


def phase2(x, w12h, w12l, w3h, w3l, out):
    o = merged(mm((w12h[...], w12l[...]), split(read_strided(x))), 256)
    u = [swap(o[p][:128], o[p][128:], 1) for p in range(2)]
    rows = [u[p][v] for p in range(2) for v in range(2)]
    u = cat([cat([rows_of(r, a, 64) for a in range(2)], 1) for r in rows], 0)
    o = merged(mm((w3h[...], w3l[...]), split(u), NT), 256)
    for p in range(2):
        for t in range(2):
            out[:, p, t] = rows_of(o[p], t, 128).reshape(16, 8, 128)


def phase3(x, w4h, w4l, w56h, w56l, l67h, l67l, out):
    o = merged(mm((w4h[...], w4l[...]), split(read_blocks(x))), 256)
    rows = []
    for p in range(2):
        pairs = [swap(rows_of(o[p], 2 * t, 64), rows_of(o[p], 2 * t + 1, 64), 64) for t in range(2)]
        rows += [cat([pairs[0][v], pairs[1][v]], 1) for v in range(2)]
    o = merged(mm((w56h[...], w56l[...]), split(cat(rows, 0)), NT), 256)
    z = mm(split(cat(o, 1)), (l67h[...], l67l[...]), NT)
    for p in range(2):
        for k in range(4):
            out[pl.ds(p * 4 + k, 64, 8), :] = z[k * 64 : (k + 1) * 64, p * 128 : (p + 1) * 128]


def phase4(x, w7h, w7l, out_real, out_imag):
    o = merged(mm((w7h[...], w7l[...]), split(read_strided(x))), 256)
    for ref, part in zip((out_real, out_imag), o):
        for t in range(2):
            ref[pl.ds(t, 128, 2), :] = rows_of(part, t, 128)


PARAMS = pltpu.CompilerParams(vmem_limit_bytes=48 << 20)
HILO512 = [jax.ShapeDtypeStruct((512, 256), BF16)] * 2
HILO256 = [jax.ShapeDtypeStruct((256, 256), BF16)] * 2


def call(kernel, name, out_shape, flops, *args, in_specs=None):
    more = {} if in_specs is None else {"in_specs": in_specs, "grid": (1,)}
    return pl.pallas_call(
        kernel,
        out_shape=out_shape,
        compiler_params=PARAMS,
        cost_estimate=pl.CostEstimate(flops=flops, bytes_accessed=4 << 20, transcendentals=0),
        name=name,
        **more,
    )(*args)


def on_device(state_real, state_imag, gate_real, gate_imag):
    shape = state_real.shape
    gr, gi = gate_real.reshape(3072, 128), gate_imag.reshape(3072, 128)
    rows = jax.ShapeDtypeStruct((512, 128), F32)
    blocks = jax.ShapeDtypeStruct((16, 2, 2, 8, 128), F32)

    def far(x):
        x = lax.all_to_all(x.reshape(16, 32, 128), "far", 0, 0, tiled=True)
        return x.reshape(16, 2, 2, 8, 128)

    def near(x):
        x = lax.all_to_all(x.reshape(64, 8, 128), "near", 0, 0, tiled=True)
        return x.reshape(512, 128)

    whole = pl.BlockSpec((256, 128), lambda i: (0, 0))
    one = lambda at: pl.BlockSpec((128, 128), lambda i: (at, 0))
    x = call(
        phase0, "phase0", blocks, 200 << 20,
        state_real.reshape(256, 128), state_imag.reshape(256, 128), gr, gi, gr, gi,
        in_specs=[whole, whole, one(0), one(0), one(3), one(3)],
    )
    x = far(x)
    first = call(prepare_first, "prepare_first", HILO512 + HILO256, 400 << 20, gr, gi)
    second = call(prepare_second, "prepare_second", HILO512 + HILO512, 800 << 20, gr, gi)
    third = call(prepare_third, "prepare_third", HILO512 + HILO512 + HILO256, 1200 << 20, gr, gi)
    fourth = call(prepare_fourth, "prepare_fourth", HILO512, 400 << 20, gr, gi)
    x = near(call(phase1, "phase1", rows, 200 << 20, x, *first))
    x = far(call(phase2, "phase2", blocks, 200 << 20, x, *second))
    x = near(call(phase3, "phase3", rows, 200 << 20, x, *third))
    flat = jax.ShapeDtypeStruct((256, 128), F32)
    real, imag = call(phase4, "phase4", [flat, flat], 200 << 20, x, *fourth)
    return real.reshape(shape), imag.reshape(shape)


def solution(mesh):
    spec = P("far", "near", None, None, None)
    return jax.shard_map(
        on_device,
        mesh=mesh,
        in_specs=(spec, spec, P(), P()),
        out_specs=(spec, spec),
        check_vma=False,
    )
```

time: 218 us -> 122 us (0.56)
  waiting for transfers between devices: 96.8 us -> 32.3 us
  matrix products: 28.6 us -> 0 us
  starting transfers between devices: 61.2 us -> 43.5 us
  Pallas kernels: 0 us -> 13.6 us
  local copies, waits for them, and re-layouts: 26.5 us -> 30.3 us
    all_to_all x8 -> x4, waiting for transfers between devices: 96.8 us -> 32.3 us  [the longest x2 23.3 us: near(): x = lax.all_to_all(x.reshape(64, 8, 128), 'near', 0, 0, tiled=True)]
    unnamed x6 -> x76, local copies, waits for them, and re-layouts: 0.01 us -> 30.3 us
    dot_general x96 -> x0, matrix products: 28.6 us -> none  [the longest x32 10.1 us: gate_top(): jnp.einsum('...hkrl,jhk->...jrl', viewed, matrix, precision=lax.Precision...]
    all_to_all x8 -> x4, starting transfers between devices: 61.2 us -> 43.5 us  [the longest x2 22 us: far(): x = lax.all_to_all(x.reshape(16, 32, 128), 'far', 0, 0, tiled=True)]
    slice x18 -> x0, local copies, waits for them, and re-layouts: 15.9 us -> none  [the longest x9 8.26 us: on_device(): gate_imag[rnd, section, which]]
    pallas_call x0 -> x9, Pallas kernels: none -> 13.6 us  [call(): pl.pallas_call(kernel, out_shape=out_shape, compiler_params=PARAMS, cost_...]
    concatenate x7 -> x0, local copies, waits for them, and re-layouts: 6.49 us -> none  [side_by_side(): both = jnp.concatenate(arrays, axis=along)]
  transfers between devices with their start and end apart: 8 -> 4, of which waited for: 8 -> 4; matrix products, arithmetic and copies ran while one was open for 7% -> 0% of each run, Pallas kernels for 0% -> 7%
where the time goes in v1:
time: 122 us; the launch traced here: 121 us
  starting transfers between devices  43.5 us (36%)
  waiting for transfers between devices  32.3 us (26%)
  local copies, waits for them, and re-layouts  30.3 us (25%)
  Pallas kernels  13.6 us (11%)
    unnamed x76, local copies, waits for them, and re-layouts  30.3 us
    all_to_all x2, waiting for transfers between devices, near(): x = lax.all_to_all(x.reshape(64, 8, 128), 'near', 0, 0, tiled=True)  23.3 us
    all_to_all x2, starting transfers between devices, far(): x = lax.all_to_all(x.reshape(16, 32, 128), 'far', 0, 0, tiled=True)  22 us
    all_to_all x2, starting transfers between devices, near(): x = lax.all_to_all(x.reshape(64, 8, 128), 'near', 0, 0, tiled=True)  21.5 us
    pallas_call x9, Pallas kernels, call(): pl.pallas_call(kernel, out_shape=out_shape, compiler_params=PARAMS, cost_...  13.6 us
    all_to_all x2, waiting for transfers between devices, far(): x = lax.all_to_all(x.reshape(16, 32, 128), 'far', 0, 0, tiled=True)  9.07 us
  transfers between devices with their start and end apart: 4, of which 4 were waited for; matrix products, arithmetic and copies ran while one was open for 0% of the time, Pallas kernels for 7%

profile of v1, /device:TPU:1, one launch (start us, length us, event | category | flops | bytes accessed | tf_op | source)
XLA Modules:
  0.0 120.6 jit_solution(12283984505090427282)
XLA Ops:
  0.6 1.4 %copy-done = f32[2,4,3,128,128]{4,3,2,1,0:T(8,128)S(1)} copy-done((f32[2,4,3,128,128]{4,3,2,1,0:T(8,128)S(1)}, f32[2,4,3,128,128]{4,3,2,1,0:T(8,128)}, u32[]{:S(2)}) %copy-start) | copy-done | bytes 1572888
  2.0 1.4 %copy-done.2 = f32[2,4,3,128,128]{4,3,2,1,0:T(8,128)S(1)} copy-done((f32[2,4,3,128,128]{4,3,2,1,0:T(8,128)S(1)}, f32[2,4,3,128,128]{4,3,2,1,0:T(8,128)}, u32[]{:S(2)}) %copy-start.2) | copy-done | bytes 1572888
  3.5 0.9 copy-done.36
  4.4 0.9 copy-done.37
  6.6 18.5 %all-to-all-start = ((f32[16,32,128]{2,1,0:T(8,128)}), f32[16,32,128]{2,1,0:T(8,128)S(1)}, u32[]{:S(2)}, u32[]{:S(2)}) async-start(f32[16,32,128]{2,1,0:T(8,128)} %bitcast.33), calls=%async_computation | async-start | bytes 524288 | tf_op jit(solution)/shard_map/all_to_all | solution.py:237
  25.1 1.7 %prepare_first.1 = (bf16[512,256]{1,0:T(8,128)(2,1)S(1)}, bf16[512,256]{1,0:T(8,128)(2,1)S(1)}, bf16[256,256]{1,0:T(8,128)(2,1)S(1)}, bf16[256,256]{1,0:T(8,128)(2,1)S(1)}) custom-call(f32[3072,128]{1,0:T(8,128)S(1)} %bitcast.16, f32[3072,128]{1,0:T(8,128)S(1)} %bitcast.22), custom_call_target="tpu_custom_call" | custom-call | flops 419430400 | bytes 4194304 | tf_op jit(solution)/shard_map/prepare_first/pallas_call | solution.py:220
  28.9 5.2 %all-to-all-done = f32[16,32,128]{2,1,0:T(8,128)S(1)} async-done(((f32[16,32,128]{2,1,0:T(8,128)}), f32[16,32,128]{2,1,0:T(8,128)S(1)}, u32[]{:S(2)}, u32[]{:S(2)}) %all-to-all-start) | async-done | bytes 262176 | tf_op jit(solution)/shard_map/all_to_all | solution.py:237
  34.0 0.9 copy-done.17
  35.0 0.9 copy-done.19
  36.8 0.9 phase1.1
  38.5 15.7 %all-to-all-start.1 = ((f32[64,8,128]{2,1,0:T(8,128)}), f32[64,8,128]{2,1,0:T(8,128)S(1)}, u32[]{:S(2)}, u32[]{:S(2)}) async-start(f32[64,8,128]{2,1,0:T(8,128)} %bitcast.29), calls=%async_computation.1 | async-start | bytes 524288 | tf_op jit(solution)/shard_map/all_to_all | solution.py:241
  54.2 2.6 %prepare_second.1 = (bf16[512,256]{1,0:T(8,128)(2,1)S(1)}, bf16[512,256]{1,0:T(8,128)(2,1)S(1)}, bf16[512,256]{1,0:T(8,128)(2,1)S(1)}, bf16[512,256]{1,0:T(8,128)(2,1)S(1)}) custom-call(f32[3072,128]{1,0:T(8,128)S(1)} %bitcast.17, f32[3072,128]{1,0:T(8,128)S(1)} %bitcast.23), custom_call_target="tpu_custom_call" | custom-call | flops 838860800 | bytes 4194304 | tf_op jit(solution)/shard_map/prepare_second/pallas_call | solution.py:220
  59.6 10.1 %all-to-all-done.1 = f32[64,8,128]{2,1,0:T(8,128)S(1)} async-done(((f32[64,8,128]{2,1,0:T(8,128)}), f32[64,8,128]{2,1,0:T(8,128)S(1)}, u32[]{:S(2)}, u32[]{:S(2)}) %all-to-all-start.1) | async-done | bytes 262176 | tf_op jit(solution)/shard_map/all_to_all | solution.py:241
  69.7 0.9 copy-done.25
  70.7 0.9 copy-done.27
  71.6 0.9 copy-done.29
  72.6 0.9 copy-done.31
  73.5 1.2 phase2.1
  75.4 3.5 %all-to-all-start.2 = ((f32[16,32,128]{2,1,0:T(8,128)}), f32[16,32,128]{2,1,0:T(8,128)S(1)}, u32[]{:S(2)}, u32[]{:S(2)}) async-start(f32[16,32,128]{2,1,0:T(8,128)} %bitcast.31), calls=%async_computation.2 | async-start | bytes 524288 | tf_op jit(solution)/shard_map/all_to_all | solution.py:237
  79.0 3.0 %prepare_third.1 = (bf16[512,256]{1,0:T(8,128)(2,1)S(1)}, bf16[512,256]{1,0:T(8,128)(2,1)S(1)}, bf16[512,256]{1,0:T(8,128)(2,1)S(1)}, bf16[512,256]{1,0:T(8,128)...) custom-call(f32[3072,128]{1,0:T(8,128)S(1)} %bitcast.18, f32[3072,128]{1,0:T(8,128)S(1)} %bitcast.24), custom_call_target="tpu_custom_call" | custom-call | flops 1258291200 | bytes 4194304 | tf_op jit(solution)/shard_map/prepare_third/pallas_call | solution.py:220
  85.5 3.9 %all-to-all-done.2 = f32[16,32,128]{2,1,0:T(8,128)S(1)} async-done(((f32[16,32,128]{2,1,0:T(8,128)}), f32[16,32,128]{2,1,0:T(8,128)S(1)}, u32[]{:S(2)}, u32[]{:S(2)}) %all-to-all-start.2) | async-done | bytes 262176 | tf_op jit(solution)/shard_map/all_to_all | solution.py:237
  89.4 0.9 copy-done.9
  90.3 0.9 copy-done.11
  91.3 0.9 copy-done.13
  92.2 0.9 copy-done.15
  94.1 1.4 %phase3.1 = f32[512,128]{1,0:T(8,128)S(1)} custom-call(f32[16,2,2,8,128]{4,3,2,1,0:T(8,128)S(1)} %bitcast.26, bf16[512,256]{1,0:T(8,128)(2,1)S(1)} %copy-done.9, bf16[512,256]{1,0:T(8,128)(2,1)S(1)} %copy-done.11, bf16[512,256]{1,0:T(8,128)(2,1)S(1)} %copy-done.13, bf16[512,256]{1,0:T(8,128)(2,1)S(1)} %copy-done.15, ...), custom_call_target="tpu_custom_call" | custom-call | flops 209715200 | bytes 4194304 | tf_op jit(solution)/shard_map/phase3/pallas_call | solution.py:220
  96.1 5.8 %all-to-all-start.3 = ((f32[64,8,128]{2,1,0:T(8,128)}), f32[64,8,128]{2,1,0:T(8,128)S(1)}, u32[]{:S(2)}, u32[]{:S(2)}) async-start(f32[64,8,128]{2,1,0:T(8,128)} %bitcast.30), calls=%async_computation.3 | async-start | bytes 524288 | tf_op jit(solution)/shard_map/all_to_all | solution.py:241
  102.0 1.1 prepare_fourth.1
  104.5 13.1 %all-to-all-done.3 = f32[64,8,128]{2,1,0:T(8,128)S(1)} async-done(((f32[64,8,128]{2,1,0:T(8,128)}), f32[64,8,128]{2,1,0:T(8,128)S(1)}, u32[]{:S(2)}, u32[]{:S(2)}) %all-to-all-start.3) | async-done | bytes 262176 | tf_op jit(solution)/shard_map/all_to_all | solution.py:241
  117.7 0.9 copy-done.21
  118.6 0.9 copy-done.23
  119.6 1.1 phase4.1
  (61 shorter events, 15.0 us)
Async XLA Ops:
  0.6 1.4 %copy-start = (f32[2,4,3,128,128]{4,3,2,1,0:T(8,128)S(1)}, f32[2,4,3,128,128]{4,3,2,1,0:T(8,128)}, u32[]{:S(2)}) copy-start(f32[2,4,3,128,128]{4,3,2,1,0:T(8,128)} %param.6) | copy-start | bytes 4718596
  2.0 1.4 %copy-start.2 = (f32[2,4,3,128,128]{4,3,2,1,0:T(8,128)S(1)}, f32[2,4,3,128,128]{4,3,2,1,0:T(8,128)}, u32[]{:S(2)}) copy-start(f32[2,4,3,128,128]{4,3,2,1,0:T(8,128)} %param.7) | copy-start | bytes 4718596
  3.4 0.9 copy-start.36
  4.4 0.9 copy-start.37
  5.3 19.8 %copy-start.1 = (f32[2,4,3,128,128]{4,3,2,1,0:T(8,128)S(1)}, f32[2,4,3,128,128]{4,3,2,1,0:T(8,128)}, u32[]{:S(2)}) copy-start(f32[2,4,3,128,128]{4,3,2,1,0:T(8,128)} %param.6) | copy-start | bytes 4718596
  5.3 19.8 %copy-start.3 = (f32[2,4,3,128,128]{4,3,2,1,0:T(8,128)S(1)}, f32[2,4,3,128,128]{4,3,2,1,0:T(8,128)}, u32[]{:S(2)}) copy-start(f32[2,4,3,128,128]{4,3,2,1,0:T(8,128)} %param.7) | copy-start | bytes 4718596
  6.6 27.4 %all-to-all-start = ((f32[16,32,128]{2,1,0:T(8,128)}), f32[16,32,128]{2,1,0:T(8,128)S(1)}, u32[]{:S(2)}, u32[]{:S(2)}) async-start(f32[16,32,128]{2,1,0:T(8,128)} %bitcast.33), calls=%async_computation | async-start | bytes 524288 | tf_op jit(solution)/shard_map/all_to_all | solution.py:237
  26.8 0.7 copy-start.16
  27.5 0.7 copy-start.18
  34.0 1.0 copy-start.17
  35.0 0.9 copy-start.19
  35.9 0.9 copy-start.35
  38.5 31.2 %all-to-all-start.1 = ((f32[64,8,128]{2,1,0:T(8,128)}), f32[64,8,128]{2,1,0:T(8,128)S(1)}, u32[]{:S(2)}, u32[]{:S(2)}) async-start(f32[64,8,128]{2,1,0:T(8,128)} %bitcast.29), calls=%async_computation.1 | async-start | bytes 524288 | tf_op jit(solution)/shard_map/all_to_all | solution.py:241
  56.8 0.7 copy-start.24
  57.5 0.7 copy-start.26
  69.7 1.0 copy-start.25
  70.7 0.9 copy-start.27
  71.6 0.9 copy-start.29
  72.6 0.9 copy-start.31
  75.4 13.9 %all-to-all-start.2 = ((f32[16,32,128]{2,1,0:T(8,128)}), f32[16,32,128]{2,1,0:T(8,128)S(1)}, u32[]{:S(2)}, u32[]{:S(2)}) async-start(f32[16,32,128]{2,1,0:T(8,128)} %bitcast.31), calls=%async_computation.2 | async-start | bytes 524288 | tf_op jit(solution)/shard_map/all_to_all | solution.py:237
  82.0 0.7 copy-start.8
  82.7 0.7 copy-start.10
  89.4 1.0 copy-start.9
  90.3 0.9 copy-start.11
  91.3 0.9 copy-start.13
  92.2 0.9 copy-start.15
  93.2 0.9 copy-start.33
  96.1 21.5 %all-to-all-start.3 = ((f32[64,8,128]{2,1,0:T(8,128)}), f32[64,8,128]{2,1,0:T(8,128)S(1)}, u32[]{:S(2)}, u32[]{:S(2)}) async-start(f32[64,8,128]{2,1,0:T(8,128)} %bitcast.30), calls=%async_computation.3 | async-start | bytes 524288 | tf_op jit(solution)/shard_map/all_to_all | solution.py:241
  103.1 0.7 copy-start.20
  103.8 0.7 copy-start.22
  117.7 1.0 copy-start.21
  118.6 0.9 copy-start.23
  (10 other events, 6.9 us)

commit v2 on v1

--- a/solution.py
+++ b/solution.py
@@ -110,10 +110,31 @@
     return gate(gr, 3 * s), gate(gi, 3 * s)
 
 
+def fetched(first, last):
+    def wrap(kernel):
+        def run(gr, gi, *rest):
+            outs, (vr, vi, sems) = rest[:-3], rest[-3:]
+            rows = pl.ds(first * 128, (last - first) * 128)
+            copies = [
+                pltpu.make_async_copy(src.at[rows], dst.at[rows], sems.at[k])
+                for k, (src, dst) in enumerate(((gr, vr), (gi, vi)))
+            ]
+            for copy in copies:
+                copy.start()
+            for copy in copies:
+                copy.wait()
+            kernel(vr, vi, *outs)
+
+        return run
+
+    return wrap
+
+
 def put(refs, x):
     refs[0][...], refs[1][...] = split(x)
 
 
+@fetched(0, 16)
 def prepare_first(gr, gi, w0h, w0l, l25h, l25l):
     sel = selector(0)
     put((w0h, w0l), cat(rows_gate(gr, gi, 0, sel), 0))
@@ -123,6 +144,7 @@
     put((l25h, l25l), big(*product(y, x)))
 
 
+@fetched(3, 12)
 def prepare_second(gr, gi, w12h, w12l, w3h, w3l):
     sel = selector(0)
     w = product(rows_gate(gr, gi, 2, sel, True), rows_gate(gr, gi, 1, sel))
@@ -130,6 +152,7 @@
     put((w3h, w3l), cat(rows_gate(gr, gi, 3, selector(1)), 0))
 
 
+@fetched(12, 24)
 def prepare_third(gr, gi, w4h, w4l, w56h, w56l, l67h, l67l):
     sel = selector(0)
     put((w4h, w4l), cat(rows_gate(gr, gi, 4, sel), 0))
@@ -139,6 +162,7 @@
     put((l67h, l67l), big(*product(low(gr, gi, 7), first)))
 
 
+@fetched(21, 24)
 def prepare_fourth(gr, gi, w7h, w7l):
     sel = selector(0)
     w = cat(rows_gate(gr, gi, 7, sel), 0)
@@ -157,8 +181,17 @@
     )
 
 
-def phase0(sr, si, g0r, g0i, g1r, g1i, out):
-    x = cat([cat([ref[pl.ds(t, 128, 2), :] for t in range(2)], 0) for ref in (sr, si)], 1)
+def phase0(sr, si, gr, gi, out, vr, vi, g0r, g0i, g1r, g1i, sems):
+    zero, one = pl.ds(0, 128), pl.ds(3 * 128, 128)
+    pairs = [
+        (sr, vr), (si, vi), (gr.at[zero], g0r), (gi.at[zero], g0i), (gr.at[one], g1r), (gi.at[one], g1i),
+    ]
+    copies = [pltpu.make_async_copy(a, b, sems.at[k]) for k, (a, b) in enumerate(pairs)]
+    for copy in copies:
+        copy.start()
+    for copy in copies:
+        copy.wait()
+    x = cat([cat([ref[pl.ds(t, 128, 2), :] for t in range(2)], 0) for ref in (vr, vi)], 1)
     x = mm(split(x), split(big(g0r[...], g0i[...])), NT)
     x = mm(split(x), split(big(g1r[...], g1i[...])), NT)
     for p in range(2):
@@ -215,8 +248,11 @@
 HILO256 = [jax.ShapeDtypeStruct((256, 256), BF16)] * 2
 
 
-def call(kernel, name, out_shape, flops, *args, in_specs=None):
-    more = {} if in_specs is None else {"in_specs": in_specs, "grid": (1,)}
+def call(kernel, name, out_shape, flops, *args, scratch=None):
+    more = {}
+    if scratch is not None:
+        in_hbm = pl.BlockSpec(memory_space=pltpu.HBM)
+        more = {"in_specs": [in_hbm] * len(args), "scratch_shapes": scratch}
     return pl.pallas_call(
         kernel,
         out_shape=out_shape,
@@ -230,6 +266,10 @@
 def on_device(state_real, state_imag, gate_real, gate_imag):
     shape = state_real.shape
     gr, gi = gate_real.reshape(3072, 128), gate_imag.reshape(3072, 128)
+    gr, gi, sr, si = (
+        pltpu.with_memory_space_constraint(a, pltpu.HBM)
+        for a in (gr, gi, state_real.reshape(256, 128), state_imag.reshape(256, 128))
+    )
     rows = jax.ShapeDtypeStruct((512, 128), F32)
     blocks = jax.ShapeDtypeStruct((16, 2, 2, 8, 128), F32)
 
@@ -241,18 +281,19 @@
         x = lax.all_to_all(x.reshape(64, 8, 128), "near", 0, 0, tiled=True)
         return x.reshape(512, 128)
 
-    whole = pl.BlockSpec((256, 128), lambda i: (0, 0))
-    one = lambda at: pl.BlockSpec((128, 128), lambda i: (at, 0))
+    state = pltpu.VMEM((256, 128), F32)
+    matrix = pltpu.VMEM((128, 128), F32)
     x = call(
         phase0, "phase0", blocks, 200 << 20,
-        state_real.reshape(256, 128), state_imag.reshape(256, 128), gr, gi, gr, gi,
-        in_specs=[whole, whole, one(0), one(0), one(3), one(3)],
-    )
+        sr, si, gr, gi,
+        scratch=[state, state] + [matrix] * 4 + [pltpu.SemaphoreType.DMA((6,))],
+    )
+    gates = [pltpu.VMEM((3072, 128), F32)] * 2 + [pltpu.SemaphoreType.DMA((2,))]
     x = far(x)
-    first = call(prepare_first, "prepare_first", HILO512 + HILO256, 400 << 20, gr, gi)
-    second = call(prepare_second, "prepare_second", HILO512 + HILO512, 800 << 20, gr, gi)
-    third = call(prepare_third, "prepare_third", HILO512 + HILO512 + HILO256, 1200 << 20, gr, gi)
-    fourth = call(prepare_fourth, "prepare_fourth", HILO512, 400 << 20, gr, gi)
+    first = call(prepare_first, "prepare_first", HILO512 + HILO256, 400 << 20, gr, gi, scratch=gates)
+    second = call(prepare_second, "prepare_second", HILO512 + HILO512, 800 << 20, gr, gi, scratch=gates)
+    third = call(prepare_third, "prepare_third", HILO512 + HILO512 + HILO256, 1200 << 20, gr, gi, scratch=gates)
+    fourth = call(prepare_fourth, "prepare_fourth", HILO512, 400 << 20, gr, gi, scratch=gates)
     x = near(call(phase1, "phase1", rows, 200 << 20, x, *first))
     x = far(call(phase2, "phase2", blocks, 200 << 20, x, *second))
     x = near(call(phase3, "phase3", rows, 200 << 20, x, *third))

time: 122 us -> 104 us (0.85); the launches traced: 121 us -> 104 us
  local copies, waits for them, and re-layouts: 30.3 us -> 0 us
  Pallas kernels: 13.6 us -> 22.9 us
  waiting for transfers between devices: 32.3 us -> 36.8 us
    unnamed x76 -> x0, local copies, waits for them, and re-layouts: 30.3 us -> none
    pallas_call x9, Pallas kernels: 13.6 us -> 22.9 us  [call(): pl.pallas_call(kernel, out_shape=out_shape, compiler_params=PARAMS, cost_...]
    all_to_all x2, waiting for transfers between devices: 9.07 us -> 11.7 us  [far(): x = lax.all_to_all(x.reshape(16, 32, 128), 'far', 0, 0, tiled=True)]
    all_to_all x2, waiting for transfers between devices: 23.3 us -> 25.2 us  [near(): x = lax.all_to_all(x.reshape(64, 8, 128), 'near', 0, 0, tiled=True)]
  transfers between devices with their start and end apart: 4 -> 4, of which waited for: 4 -> 4; matrix products, arithmetic and copies ran while one was open for 0% -> 0% of each run, Pallas kernels for 7% -> 13%
where the time goes in v2:
time: 104 us
  starting transfers between devices  43.5 us (42%)
  waiting for transfers between devices  36.8 us (35%)
  Pallas kernels  22.9 us (22%)
    all_to_all x2, waiting for transfers between devices, near(): x = lax.all_to_all(x.reshape(64, 8, 128), 'near', 0, 0, tiled=True)  25.2 us
    pallas_call x9, Pallas kernels, call(): pl.pallas_call(kernel, out_shape=out_shape, compiler_params=PARAMS, cost_...  22.9 us
    all_to_all x2, starting transfers between devices, far(): x = lax.all_to_all(x.reshape(16, 32, 128), 'far', 0, 0, tiled=True)  22 us
    all_to_all x2, starting transfers between devices, near(): x = lax.all_to_all(x.reshape(64, 8, 128), 'near', 0, 0, tiled=True)  21.5 us
    all_to_all x2, waiting for transfers between devices, far(): x = lax.all_to_all(x.reshape(16, 32, 128), 'far', 0, 0, tiled=True)  11.7 us
  transfers between devices with their start and end apart: 4, of which 4 were waited for; matrix products, arithmetic and copies ran while one was open for 0% of the time, Pallas kernels for 13%

profile of v2, /device:TPU:1, one launch (start us, length us, event | category | flops | bytes accessed | tf_op | source)
XLA Modules:
  0.0 103.9 jit_solution(3207198246889396545)
XLA Ops:
  0.6 2.5 %phase0.1 = f32[16,2,2,8,128]{4,3,2,1,0:T(8,128)} custom-call(f32[256,128]{1,0:T(8,128)} %bitcast.28, f32[256,128]{1,0:T(8,128)} %bitcast.29, f32[3072,128]{1,0:T(8,128)} %bitcast.18, f32[3072,128]{1,0:T(8,128)} %bitcast.23), custom_call_target="tpu_custom_call" | custom-call | flops 209715200 | bytes 4194304 | tf_op jit(solution)/shard_map/phase0/pallas_call | solution.py:256
  3.1 18.5 %all-to-all-start = ((f32[16,32,128]{2,1,0:T(8,128)}), f32[16,32,128]{2,1,0:T(8,128)S(1)}, u32[]{:S(2)}, u32[]{:S(2)}) async-start(f32[16,32,128]{2,1,0:T(8,128)} %bitcast.4), calls=%async_computation | async-start | bytes 524288 | tf_op jit(solution)/shard_map/all_to_all | solution.py:277
  21.6 3.2 %prepare_first.1 = (bf16[512,256]{1,0:T(8,128)(2,1)S(1)}, bf16[512,256]{1,0:T(8,128)(2,1)S(1)}, bf16[256,256]{1,0:T(8,128)(2,1)S(1)}, bf16[256,256]{1,0:T(8,128)(2,1)S(1)}) custom-call(f32[3072,128]{1,0:T(8,128)} %bitcast.19, f32[3072,128]{1,0:T(8,128)} %bitcast.24), custom_call_target="tpu_custom_call" | custom-call | flops 419430400 | bytes 4194304 | tf_op jit(solution)/shard_map/prepare_first/pallas_call | solution.py:256
  24.8 5.7 %all-to-all-done = f32[16,32,128]{2,1,0:T(8,128)S(1)} async-done(((f32[16,32,128]{2,1,0:T(8,128)}), f32[16,32,128]{2,1,0:T(8,128)S(1)}, u32[]{:S(2)}, u32[]{:S(2)}) %all-to-all-start) | async-done | bytes 262176 | tf_op jit(solution)/shard_map/all_to_all | solution.py:277
  30.5 1.7 %phase1.1 = f32[512,128]{1,0:T(8,128)} custom-call(f32[16,2,2,8,128]{4,3,2,1,0:T(8,128)S(1)} %bitcast.15, bf16[512,256]{1,0:T(8,128)(2,1)S(1)} %get-tuple-element.20.w0h, bf16[512,256]{1,0:T(8,128)(2,1)S(1)} %get-tuple-element.21.w0l, bf16[256,256]{1,0:T(8,128)(2,1)S(1)} %get-tuple-element.22.l25h, bf16[256,256]{1,0:T(8,128)(2,1)S(1)} %get-tuple-element.23.l25l), custom_call_target="tpu_custom_call" | custom-call | flops 209715200 | bytes 4194304 | tf_op jit(solution)/shard_map/phase1/pallas_call | solution.py:256
  32.2 15.7 %all-to-all-start.1 = ((f32[64,8,128]{2,1,0:T(8,128)}), f32[64,8,128]{2,1,0:T(8,128)S(1)}, u32[]{:S(2)}, u32[]{:S(2)}) async-start(f32[64,8,128]{2,1,0:T(8,128)} %bitcast.6), calls=%async_computation.1 | async-start | bytes 524288 | tf_op jit(solution)/shard_map/all_to_all | solution.py:281
  47.9 3.9 %prepare_second.1 = (bf16[512,256]{1,0:T(8,128)(2,1)S(1)}, bf16[512,256]{1,0:T(8,128)(2,1)S(1)}, bf16[512,256]{1,0:T(8,128)(2,1)S(1)}, bf16[512,256]{1,0:T(8,128)(2,1)S(1)}) custom-call(f32[3072,128]{1,0:T(8,128)} %bitcast.20, f32[3072,128]{1,0:T(8,128)} %bitcast.25), custom_call_target="tpu_custom_call" | custom-call | flops 838860800 | bytes 4194304 | tf_op jit(solution)/shard_map/prepare_second/pallas_call | solution.py:256
  51.8 11.7 %all-to-all-done.1 = f32[64,8,128]{2,1,0:T(8,128)S(1)} async-done(((f32[64,8,128]{2,1,0:T(8,128)}), f32[64,8,128]{2,1,0:T(8,128)S(1)}, u32[]{:S(2)}, u32[]{:S(2)}) %all-to-all-start.1) | async-done | bytes 262176 | tf_op jit(solution)/shard_map/all_to_all | solution.py:281
  63.4 1.9 %phase2.1 = f32[16,2,2,8,128]{4,3,2,1,0:T(8,128)} custom-call(f32[512,128]{1,0:T(8,128)S(1)} %bitcast.17, bf16[512,256]{1,0:T(8,128)(2,1)S(1)} %get-tuple-element.24.w12h, bf16[512,256]{1,0:T(8,128)(2,1)S(1)} %get-tuple-element.25.w12l, bf16[512,256]{1,0:T(8,128)(2,1)S(1)} %get-tuple-element.26.w3h, bf16[512,256]{1,0:T(8,128)(2,1)S(1)} %get-tuple-element.27.w3l), custom_call_target="tpu_custom_call" | custom-call | flops 209715200 | bytes 4194304 | tf_op jit(solution)/shard_map/phase2/pallas_call | solution.py:256
  65.3 3.5 %all-to-all-start.2 = ((f32[16,32,128]{2,1,0:T(8,128)}), f32[16,32,128]{2,1,0:T(8,128)S(1)}, u32[]{:S(2)}, u32[]{:S(2)}) async-start(f32[16,32,128]{2,1,0:T(8,128)} %bitcast.8), calls=%async_computation.2 | async-start | bytes 524288 | tf_op jit(solution)/shard_map/all_to_all | solution.py:277
  68.9 4.4 %prepare_third.1 = (bf16[512,256]{1,0:T(8,128)(2,1)S(1)}, bf16[512,256]{1,0:T(8,128)(2,1)S(1)}, bf16[512,256]{1,0:T(8,128)(2,1)S(1)}, bf16[512,256]{1,0:T(8,128)...) custom-call(f32[3072,128]{1,0:T(8,128)} %bitcast.21, f32[3072,128]{1,0:T(8,128)} %bitcast.26), custom_call_target="tpu_custom_call" | custom-call | flops 1258291200 | bytes 4194304 | tf_op jit(solution)/shard_map/prepare_third/pallas_call | solution.py:256
  73.3 6.0 %all-to-all-done.2 = f32[16,32,128]{2,1,0:T(8,128)S(1)} async-done(((f32[16,32,128]{2,1,0:T(8,128)}), f32[16,32,128]{2,1,0:T(8,128)S(1)}, u32[]{:S(2)}, u32[]{:S(2)}) %all-to-all-start.2) | async-done | bytes 262176 | tf_op jit(solution)/shard_map/all_to_all | solution.py:277
  79.3 2.1 %phase3.1 = f32[512,128]{1,0:T(8,128)} custom-call(f32[16,2,2,8,128]{4,3,2,1,0:T(8,128)S(1)} %bitcast.14, bf16[512,256]{1,0:T(8,128)(2,1)S(1)} %get-tuple-element.28.w4h, bf16[512,256]{1,0:T(8,128)(2,1)S(1)} %get-tuple-element.29.w4l, bf16[512,256]{1,0:T(8,128)(2,1)S(1)} %get-tuple-element.30.w56h, bf16[512,256]{1,0:T(8,128)(2,1)S(1)} %get-tuple-element.31.w56l, ...), custom_call_target="tpu_custom_call" | custom-call | flops 209715200 | bytes 4194304 | tf_op jit(solution)/shard_map/phase3/pallas_call | solution.py:256
  81.3 5.8 %all-to-all-start.3 = ((f32[64,8,128]{2,1,0:T(8,128)}), f32[64,8,128]{2,1,0:T(8,128)S(1)}, u32[]{:S(2)}, u32[]{:S(2)}) async-start(f32[64,8,128]{2,1,0:T(8,128)} %bitcast.10), calls=%async_computation.3 | async-start | bytes 524288 | tf_op jit(solution)/shard_map/all_to_all | solution.py:281
  87.2 2.1 %prepare_fourth.1 = (bf16[512,256]{1,0:T(8,128)(2,1)S(1)}, bf16[512,256]{1,0:T(8,128)(2,1)S(1)}) custom-call(f32[3072,128]{1,0:T(8,128)} %bitcast.22, f32[3072,128]{1,0:T(8,128)} %bitcast.27), custom_call_target="tpu_custom_call" | custom-call | flops 419430400 | bytes 4194304 | tf_op jit(solution)/shard_map/prepare_fourth/pallas_call | solution.py:256
  89.3 13.5 %all-to-all-done.3 = f32[64,8,128]{2,1,0:T(8,128)S(1)} async-done(((f32[64,8,128]{2,1,0:T(8,128)}), f32[64,8,128]{2,1,0:T(8,128)S(1)}, u32[]{:S(2)}, u32[]{:S(2)}) %all-to-all-start.3) | async-done | bytes 262176 | tf_op jit(solution)/shard_map/all_to_all | solution.py:281
  102.8 1.1 %phase4.1 = (f32[256,128]{1,0:T(8,128)}, f32[256,128]{1,0:T(8,128)}) custom-call(f32[512,128]{1,0:T(8,128)S(1)} %bitcast.16, bf16[512,256]{1,0:T(8,128)(2,1)S(1)} %get-tuple-element.34.w7h, bf16[512,256]{1,0:T(8,128)(2,1)S(1)} %get-tuple-element.35.w7l), custom_call_target="tpu_custom_call" | custom-call | flops 209715200 | bytes 4194304 | tf_op jit(solution)/shard_map/phase4/pallas_call | solution.py:256
Async XLA Ops:
  3.1 27.4 %all-to-all-start = ((f32[16,32,128]{2,1,0:T(8,128)}), f32[16,32,128]{2,1,0:T(8,128)S(1)}, u32[]{:S(2)}, u32[]{:S(2)}) async-start(f32[16,32,128]{2,1,0:T(8,128)} %bitcast.4), calls=%async_computation | async-start | bytes 524288 | tf_op jit(solution)/shard_map/all_to_all | solution.py:277
  32.2 31.3 %all-to-all-start.1 = ((f32[64,8,128]{2,1,0:T(8,128)}), f32[64,8,128]{2,1,0:T(8,128)S(1)}, u32[]{:S(2)}, u32[]{:S(2)}) async-start(f32[64,8,128]{2,1,0:T(8,128)} %bitcast.6), calls=%async_computation.1 | async-start | bytes 524288 | tf_op jit(solution)/shard_map/all_to_all | solution.py:281
  65.3 13.9 %all-to-all-start.2 = ((f32[16,32,128]{2,1,0:T(8,128)}), f32[16,32,128]{2,1,0:T(8,128)S(1)}, u32[]{:S(2)}, u32[]{:S(2)}) async-start(f32[16,32,128]{2,1,0:T(8,128)} %bitcast.8), calls=%async_computation.2 | async-start | bytes 524288 | tf_op jit(solution)/shard_map/all_to_all | solution.py:277
  81.3 21.5 %all-to-all-start.3 = ((f32[64,8,128]{2,1,0:T(8,128)}), f32[64,8,128]{2,1,0:T(8,128)S(1)}, u32[]{:S(2)}, u32[]{:S(2)}) async-start(f32[64,8,128]{2,1,0:T(8,128)} %bitcast.10), calls=%async_computation.3 | async-start | bytes 524288 | tf_op jit(solution)/shard_map/all_to_all | solution.py:281

commit v3 on v2

--- a/solution.py
+++ b/solution.py
@@ -71,6 +71,22 @@
 
 def odd_even(ref, at):
     return cat([ref[pl.ds(at * 128 + t, 64, 2), :] for t in range(2)], 0)
+
+
+def rows_gate_plain(gr, gi, s):
+    m = [odd_even(ref, 3 * s + 1) for ref in (gr, gi)]
+    c = split(cat([gate(ref, 3 * s + 2) for ref in (gr, gi)], 0))
+    zero = jnp.zeros((64, 128), F32)
+    real, imag = [], []
+    for t in range(2):
+        diagonal = []
+        for part in range(2):
+            x = rows_of(m[part], t, 64)
+            diagonal.append(cat([cat([x, zero], 1), cat([zero, x], 1)], 0))
+        wr, wi = merged(mm(c, split(cat(diagonal, 1))), 128)
+        real.append(wr)
+        imag.append(wi)
+    return cat(real, 0), cat(imag, 0)
 
 
 def rows_gate(gr, gi, s, sel, top_moved=False):
@@ -135,36 +151,27 @@
 
 
 @fetched(0, 16)
-def prepare_first(gr, gi, w0h, w0l, l25h, l25l):
+def prepare_first(gr, gi, l01h, l01l, w0h, w0l, l25h, l25l, w12h, w12l, w3h, w3l):
     sel = selector(0)
-    put((w0h, w0l), cat(rows_gate(gr, gi, 0, sel), 0))
+    put((l01h, l01l), big(*product(low(gr, gi, 1), low(gr, gi, 0))))
+    put((w0h, w0l), cat(rows_gate_plain(gr, gi, 0), 0))
     first = tuple(columns_moved(a, sel) for a in low(gr, gi, 2))
     x = product(low(gr, gi, 3), first)
     y = product((odd_even(gr, 15), odd_even(gi, 15)), low(gr, gi, 4))
     put((l25h, l25l), big(*product(y, x)))
-
-
-@fetched(3, 12)
-def prepare_second(gr, gi, w12h, w12l, w3h, w3l):
-    sel = selector(0)
     w = product(rows_gate(gr, gi, 2, sel, True), rows_gate(gr, gi, 1, sel))
     put((w12h, w12l), cat(w, 0))
     put((w3h, w3l), cat(rows_gate(gr, gi, 3, selector(1)), 0))
 
 
 @fetched(12, 24)
-def prepare_third(gr, gi, w4h, w4l, w56h, w56l, l67h, l67l):
+def prepare_second(gr, gi, w4h, w4l, w56h, w56l, l67h, l67l, w7h, w7l):
     sel = selector(0)
     put((w4h, w4l), cat(rows_gate(gr, gi, 4, sel), 0))
     w = product(rows_gate(gr, gi, 6, sel, True), rows_gate(gr, gi, 5, sel))
     put((w56h, w56l), cat(w, 0))
     first = tuple(columns_moved(a, sel) for a in low(gr, gi, 6))
     put((l67h, l67l), big(*product(low(gr, gi, 7), first)))
-
-
-@fetched(21, 24)
-def prepare_fourth(gr, gi, w7h, w7l):
-    sel = selector(0)
     w = cat(rows_gate(gr, gi, 7, sel), 0)
     put((w7h, w7l), cat([columns_moved(w[:, :128], sel), columns_moved(w[:, 128:], sel)], 1))
 
@@ -181,26 +188,20 @@
     )
 
 
-def phase0(sr, si, gr, gi, out, vr, vi, g0r, g0i, g1r, g1i, sems):
-    zero, one = pl.ds(0, 128), pl.ds(3 * 128, 128)
-    pairs = [
-        (sr, vr), (si, vi), (gr.at[zero], g0r), (gi.at[zero], g0i), (gr.at[one], g1r), (gi.at[one], g1i),
+def phase0(sr, si, out, sems):
+    copies = [
+        pltpu.make_async_copy(ref, out.at[:, p], sems.at[p]) for p, ref in enumerate((sr, si))
     ]
-    copies = [pltpu.make_async_copy(a, b, sems.at[k]) for k, (a, b) in enumerate(pairs)]
     for copy in copies:
         copy.start()
     for copy in copies:
         copy.wait()
-    x = cat([cat([ref[pl.ds(t, 128, 2), :] for t in range(2)], 0) for ref in (vr, vi)], 1)
-    x = mm(split(x), split(big(g0r[...], g0i[...])), NT)
-    x = mm(split(x), split(big(g1r[...], g1i[...])), NT)
-    for p in range(2):
-        for t in range(2):
-            out[:, p, t] = x[t * 128 : (t + 1) * 128, p * 128 : (p + 1) * 128].reshape(16, 8, 128)
-
-
-def phase1(x, w0h, w0l, l25h, l25l, out):
-    o = merged(mm((w0h[...], w0l[...]), split(read_blocks(x))), 256)
+
+
+def phase1(x, l01h, l01l, w0h, w0l, l25h, l25l, out):
+    y = cat([x[:, p].reshape(256, 128) for p in range(2)], 1)
+    y = mm(split(y), (l01h[...], l01l[...]), NT)
+    o = merged(mm((w0h[...], w0l[...]), split(y)), 256)
     u = [swap(o[p][:128], o[p][128:], 1) for p in range(2)]
     rows = [u[p][v] for p in range(2) for v in range(2)]
     u = cat([cat([rows_of(r, f, 64) for r in rows], 0) for f in range(2)], 1)
@@ -248,11 +249,13 @@
 HILO256 = [jax.ShapeDtypeStruct((256, 256), BF16)] * 2
 
 
-def call(kernel, name, out_shape, flops, *args, scratch=None):
+def call(kernel, name, out_shape, flops, *args, scratch=None, out_specs=None):
     more = {}
     if scratch is not None:
         in_hbm = pl.BlockSpec(memory_space=pltpu.HBM)
         more = {"in_specs": [in_hbm] * len(args), "scratch_shapes": scratch}
+    if out_specs is not None:
+        more["out_specs"] = out_specs
     return pl.pallas_call(
         kernel,
         out_shape=out_shape,
@@ -265,40 +268,43 @@
 
 def on_device(state_real, state_imag, gate_real, gate_imag):
     shape = state_real.shape
-    gr, gi = gate_real.reshape(3072, 128), gate_imag.reshape(3072, 128)
-    gr, gi, sr, si = (
+    sr, si, gr, gi = (
         pltpu.with_memory_space_constraint(a, pltpu.HBM)
-        for a in (gr, gi, state_real.reshape(256, 128), state_imag.reshape(256, 128))
+        for a in (
+            state_real.reshape(16, 16, 128), state_imag.reshape(16, 16, 128),
+            gate_real.reshape(3072, 128), gate_imag.reshape(3072, 128),
+        )
     )
     rows = jax.ShapeDtypeStruct((512, 128), F32)
     blocks = jax.ShapeDtypeStruct((16, 2, 2, 8, 128), F32)
 
     def far(x):
-        x = lax.all_to_all(x.reshape(16, 32, 128), "far", 0, 0, tiled=True)
-        return x.reshape(16, 2, 2, 8, 128)
+        return lax.all_to_all(x.reshape(16, 32, 128), "far", 0, 0, tiled=True)
 
     def near(x):
         x = lax.all_to_all(x.reshape(64, 8, 128), "near", 0, 0, tiled=True)
         return x.reshape(512, 128)
 
-    state = pltpu.VMEM((256, 128), F32)
-    matrix = pltpu.VMEM((128, 128), F32)
     x = call(
-        phase0, "phase0", blocks, 200 << 20,
-        sr, si, gr, gi,
-        scratch=[state, state] + [matrix] * 4 + [pltpu.SemaphoreType.DMA((6,))],
+        phase0, "phase0", jax.ShapeDtypeStruct((16, 2, 16, 128), F32), 1 << 20, sr, si,
+        scratch=[pltpu.SemaphoreType.DMA((2,))], out_specs=pl.BlockSpec(memory_space=pltpu.HBM),
     )
     gates = [pltpu.VMEM((3072, 128), F32)] * 2 + [pltpu.SemaphoreType.DMA((2,))]
     x = far(x)
-    first = call(prepare_first, "prepare_first", HILO512 + HILO256, 400 << 20, gr, gi, scratch=gates)
-    second = call(prepare_second, "prepare_second", HILO512 + HILO512, 800 << 20, gr, gi, scratch=gates)
-    third = call(prepare_third, "prepare_third", HILO512 + HILO512 + HILO256, 1200 << 20, gr, gi, scratch=gates)
-    fourth = call(prepare_fourth, "prepare_fourth", HILO512, 400 << 20, gr, gi, scratch=gates)
-    x = near(call(phase1, "phase1", rows, 200 << 20, x, *first))
-    x = far(call(phase2, "phase2", blocks, 200 << 20, x, *second))
-    x = near(call(phase3, "phase3", rows, 200 << 20, x, *third))
+    first = call(
+        prepare_first, "prepare_first", HILO256 + HILO512 + HILO256 + HILO512 + HILO512, 1200 << 20,
+        gr, gi, scratch=gates,
+    )
+    x = near(call(phase1, "phase1", rows, 200 << 20, x.reshape(16, 2, 16, 128), *first[:6]))
+    x = far(call(phase2, "phase2", blocks, 200 << 20, x, *first[6:]))
+    second = call(
+        prepare_second, "prepare_second", HILO512 + HILO512 + HILO256 + HILO512, 1600 << 20,
+        gr, gi, scratch=gates,
+    )
+    x = x.reshape(16, 2, 2, 8, 128)
+    x = near(call(phase3, "phase3", rows, 200 << 20, x, *second[:6]))
     flat = jax.ShapeDtypeStruct((256, 128), F32)
-    real, imag = call(phase4, "phase4", [flat, flat], 200 << 20, x, *fourth)
+    real, imag = call(phase4, "phase4", [flat, flat], 200 << 20, x, *second[6:])
     return real.reshape(shape), imag.reshape(shape)
 
 

time: 104 us -> 109 us (1.048)
  blocking collectives: 0 us -> 51.7 us
  waiting for transfers between devices: 36.8 us -> 9.25 us
  starting transfers between devices: 43.5 us -> 22 us
  Pallas kernels: 22.9 us -> 24.8 us
    all_to_all x0 -> x2, blocking collectives: none -> 51.7 us  [near(): x = lax.all_to_all(x.reshape(64, 8, 128), 'near', 0, 0, tiled=True)]
    all_to_all x4 -> x2, waiting for transfers between devices: 36.8 us -> 9.25 us  [far(): return lax.all_to_all(x.reshape(16, 32, 128), 'far', 0, 0, tiled=True)]
    all_to_all x4 -> x2, starting transfers between devices: 43.5 us -> 22 us  [far(): return lax.all_to_all(x.reshape(16, 32, 128), 'far', 0, 0, tiled=True)]
    pallas_call x9 -> x7, Pallas kernels: 22.9 us -> 24.8 us  [call(): pl.pallas_call(kernel, out_shape=out_shape, compiler_params=PARAMS, cost_...]
  transfers between devices with their start and end apart: 4 -> 2, of which waited for: 4 -> 2; matrix products, arithmetic and copies ran while one was open for 0% -> 0% of each run, Pallas kernels for 13% -> 9%
where the time goes in v3:
time: 109 us
  blocking collectives  51.7 us (47%)
  Pallas kernels  24.8 us (23%)
  starting transfers between devices  22 us (20%)
  waiting for transfers between devices  9.25 us (8%)
    all_to_all x2, blocking collectives, near(): x = lax.all_to_all(x.reshape(64, 8, 128), 'near', 0, 0, tiled=True)  51.7 us
    pallas_call x7, Pallas kernels, call(): pl.pallas_call(kernel, out_shape=out_shape, compiler_params=PARAMS, cost_...  24.8 us
    all_to_all x2, starting transfers between devices, far(): return lax.all_to_all(x.reshape(16, 32, 128), 'far', 0, 0, tiled=True)  22 us
    all_to_all x2, waiting for transfers between devices, far(): return lax.all_to_all(x.reshape(16, 32, 128), 'far', 0, 0, tiled=True)  9.25 us
  transfers between devices with their start and end apart: 2, of which 2 were waited for; matrix products, arithmetic and copies ran while one was open for 0% of the time, Pallas kernels for 9%

profile of v3, /device:TPU:1, one launch (start us, length us, event | category | flops | bytes accessed | tf_op | source)
XLA Modules:
  0.0 108.5 jit_solution(16692202177372067746)
XLA Ops:
  0.6 9.1 %phase0.1 = f32[16,2,16,128]{3,2,1,0:T(8,128)} custom-call(f32[16,16,128]{2,1,0:T(8,128)} %bitcast.20, f32[16,16,128]{2,1,0:T(8,128)} %bitcast.21), custom_call_target="tpu_custom_call" | custom-call | flops 1048576 | bytes 4194304 | tf_op jit(solution)/shard_map/phase0/pallas_call | solution.py:259
  9.7 18.5 %all-to-all-start = ((f32[16,32,128]{2,1,0:T(8,128)}), f32[16,32,128]{2,1,0:T(8,128)S(1)}, u32[]{:S(2)}, u32[]{:S(2)}) async-start(f32[16,32,128]{2,1,0:T(8,128)} %bitcast.2), calls=%async_computation | async-start | bytes 524288 | tf_op jit(solution)/shard_map/all_to_all | solution.py:282
  28.2 4.9 %prepare_first.1 = (bf16[256,256]{1,0:T(8,128)(2,1)S(1)}, bf16[256,256]{1,0:T(8,128)(2,1)S(1)}, bf16[512,256]{1,0:T(8,128)(2,1)S(1)}, bf16[512,256]{1,0:T(8,128)...) custom-call(f32[3072,128]{1,0:T(8,128)} %bitcast.22, ...), custom_call_target="tpu_custom_call" | custom-call | flops 1258291200 | bytes 4194304 | tf_op jit(solution)/shard_map/prepare_first/pallas_call | solution.py:259
  33.1 4.0 %all-to-all-done = f32[16,32,128]{2,1,0:T(8,128)S(1)} async-done(((f32[16,32,128]{2,1,0:T(8,128)}), f32[16,32,128]{2,1,0:T(8,128)S(1)}, u32[]{:S(2)}, u32[]{:S(2)}) %all-to-all-start) | async-done | bytes 262176 | tf_op jit(solution)/shard_map/all_to_all | solution.py:282
  37.1 1.4 %phase1.1 = f32[512,128]{1,0:T(8,128)S(1)} custom-call(f32[16,2,16,128]{3,2,1,0:T(8,128)S(1)} %bitcast.17, bf16[256,256]{1,0:T(8,128)(2,1)S(1)} %get-tuple-element.22.l01h, bf16[256,256]{1,0:T(8,128)(2,1)S(1)} %get-tuple-element.23.l01l, bf16[512,256]{1,0:T(8,128)(2,1)S(1)} %get-tuple-element.24.w0h, bf16[512,256]{1,0:T(8,128)(2,1)S(1)} %get-tuple-element.25.w0l, ...), custom_call_target="tpu_custom_call" | custom-call | flops 209715200 | bytes 4194304 | tf_op jit(solution)/shard_map/phase1/pallas_call | solution.py:259
  38.5 31.0 %all_to_all.20 = f32[64,8,128]{2,1,0:T(8,128)S(1)} all-to-all(f32[64,8,128]{2,1,0:T(8,128)S(1)} %bitcast.18), channel_id=1, replica_groups=mesh['far'=16,'near'=64] {'near'}, dimensions={0} | all-to-all | bytes 524288 | tf_op jit(solution)/shard_map/all_to_all | solution.py:285
  69.5 1.9 %phase2.1 = f32[16,2,2,8,128]{4,3,2,1,0:T(8,128)} custom-call(f32[512,128]{1,0:T(8,128)S(1)} %bitcast.19, bf16[512,256]{1,0:T(8,128)(2,1)S(1)} %get-tuple-element.28.w12h, bf16[512,256]{1,0:T(8,128)(2,1)S(1)} %get-tuple-element.29.w12l, bf16[512,256]{1,0:T(8,128)(2,1)S(1)} %get-tuple-element.30.w3h, bf16[512,256]{1,0:T(8,128)(2,1)S(1)} %get-tuple-element.31.w3l), custom_call_target="tpu_custom_call" | custom-call | flops 209715200 | bytes 4194304 | tf_op jit(solution)/shard_map/phase2/pallas_call | solution.py:259
  71.4 3.5 %all-to-all-start.2 = ((f32[16,32,128]{2,1,0:T(8,128)}), f32[16,32,128]{2,1,0:T(8,128)S(1)}, u32[]{:S(2)}, u32[]{:S(2)}) async-start(f32[16,32,128]{2,1,0:T(8,128)} %bitcast.8), calls=%async_computation.2 | async-start | bytes 524288 | tf_op jit(solution)/shard_map/all_to_all | solution.py:282
  75.0 5.1 %prepare_second.1 = (bf16[512,256]{1,0:T(8,128)(2,1)S(1)}, bf16[512,256]{1,0:T(8,128)(2,1)S(1)}, bf16[512,256]{1,0:T(8,128)(2,1)S(1)}, bf16[512,256]{1,0:T(8,128...) custom-call(f32[3072,128]{1,0:T(8,128)} %bitcast.23, ...), custom_call_target="tpu_custom_call" | custom-call | flops 1677721600 | bytes 4194304 | tf_op jit(solution)/shard_map/prepare_second/pallas_call | solution.py:259
  80.1 5.3 %all-to-all-done.2 = f32[16,32,128]{2,1,0:T(8,128)S(1)} async-done(((f32[16,32,128]{2,1,0:T(8,128)}), f32[16,32,128]{2,1,0:T(8,128)S(1)}, u32[]{:S(2)}, u32[]{:S(2)}) %all-to-all-start.2) | async-done | bytes 262176 | tf_op jit(solution)/shard_map/all_to_all | solution.py:282
  85.4 1.4 %phase3.1 = f32[512,128]{1,0:T(8,128)S(1)} custom-call(f32[16,2,2,8,128]{4,3,2,1,0:T(8,128)S(1)} %bitcast.14, bf16[512,256]{1,0:T(8,128)(2,1)S(1)} %get-tuple-element.32.w4h, bf16[512,256]{1,0:T(8,128)(2,1)S(1)} %get-tuple-element.33.w4l, bf16[512,256]{1,0:T(8,128)(2,1)S(1)} %get-tuple-element.34.w56h, bf16[512,256]{1,0:T(8,128)(2,1)S(1)} %get-tuple-element.35.w56l, ...), custom_call_target="tpu_custom_call" | custom-call | flops 209715200 | bytes 4194304 | tf_op jit(solution)/shard_map/phase3/pallas_call | solution.py:259
  86.8 20.7 %all_to_all.21 = f32[64,8,128]{2,1,0:T(8,128)S(1)} all-to-all(f32[64,8,128]{2,1,0:T(8,128)S(1)} %bitcast.15), channel_id=1, replica_groups=mesh['far'=16,'near'=64] {'near'}, dimensions={0} | all-to-all | bytes 524288 | tf_op jit(solution)/shard_map/all_to_all | solution.py:285
  107.5 1.1 %phase4.1 = (f32[256,128]{1,0:T(8,128)}, f32[256,128]{1,0:T(8,128)}) custom-call(f32[512,128]{1,0:T(8,128)S(1)} %bitcast.16, bf16[512,256]{1,0:T(8,128)(2,1)S(1)} %get-tuple-element.38.w7h, bf16[512,256]{1,0:T(8,128)(2,1)S(1)} %get-tuple-element.39.w7l), custom_call_target="tpu_custom_call" | custom-call | flops 209715200 | bytes 4194304 | tf_op jit(solution)/shard_map/phase4/pallas_call | solution.py:259
Async XLA Ops:
  9.7 27.4 %all-to-all-start = ((f32[16,32,128]{2,1,0:T(8,128)}), f32[16,32,128]{2,1,0:T(8,128)S(1)}, u32[]{:S(2)}, u32[]{:S(2)}) async-start(f32[16,32,128]{2,1,0:T(8,128)} %bitcast.2), calls=%async_computation | async-start | bytes 524288 | tf_op jit(solution)/shard_map/all_to_all | solution.py:282
  71.4 13.9 %all-to-all-start.2 = ((f32[16,32,128]{2,1,0:T(8,128)}), f32[16,32,128]{2,1,0:T(8,128)S(1)}, u32[]{:S(2)}, u32[]{:S(2)}) async-start(f32[16,32,128]{2,1,0:T(8,128)} %bitcast.8), calls=%async_computation.2 | async-start | bytes 524288 | tf_op jit(solution)/shard_map/all_to_all | solution.py:282

commit v4 on v3

--- a/solution.py
+++ b/solution.py
@@ -188,14 +188,14 @@
     )
 
 
-def phase0(sr, si, out, sems):
-    copies = [
-        pltpu.make_async_copy(ref, out.at[:, p], sems.at[p]) for p, ref in enumerate((sr, si))
-    ]
+def phase0(sr, si, out, vr, vi, sems):
+    pairs = [(sr, vr), (si, vi)]
+    copies = [pltpu.make_async_copy(a, b, sems.at[p]) for p, (a, b) in enumerate(pairs)]
     for copy in copies:
         copy.start()
-    for copy in copies:
+    for p, copy in enumerate(copies):
         copy.wait()
+        out[:, p] = pairs[p][1][...]
 
 
 def phase1(x, l01h, l01l, w0h, w0l, l25h, l25l, out):
@@ -287,7 +287,7 @@
 
     x = call(
         phase0, "phase0", jax.ShapeDtypeStruct((16, 2, 16, 128), F32), 1 << 20, sr, si,
-        scratch=[pltpu.SemaphoreType.DMA((2,))], out_specs=pl.BlockSpec(memory_space=pltpu.HBM),
+        scratch=[pltpu.VMEM((16, 16, 128), F32)] * 2 + [pltpu.SemaphoreType.DMA((2,))],
     )
     gates = [pltpu.VMEM((3072, 128), F32)] * 2 + [pltpu.SemaphoreType.DMA((2,))]
     x = far(x)

time: 109 us -> 102 us (0.936)
  Pallas kernels: 24.8 us -> 17.5 us
    pallas_call x7, Pallas kernels: 24.8 us -> 17.5 us  [call(): pl.pallas_call(kernel, out_shape=out_shape, compiler_params=PARAMS, cost_...]
  transfers between devices with their start and end apart: 2 -> 2, of which waited for: 2 -> 2; matrix products, arithmetic and copies ran while one was open for 0% -> 0% of each run, Pallas kernels for 9% -> 10%
where the time goes in v4:
time: 102 us; the launch traced here: 101 us
  blocking collectives  51.7 us (51%)
  starting transfers between devices  22 us (22%)
  Pallas kernels  17.5 us (17%)
  waiting for transfers between devices  9.25 us (9%)
    all_to_all x2, blocking collectives, near(): x = lax.all_to_all(x.reshape(64, 8, 128), 'near', 0, 0, tiled=True)  51.7 us
    all_to_all x2, starting transfers between devices, far(): return lax.all_to_all(x.reshape(16, 32, 128), 'far', 0, 0, tiled=True)  22 us
    pallas_call x7, Pallas kernels, call(): pl.pallas_call(kernel, out_shape=out_shape, compiler_params=PARAMS, cost_...  17.5 us
    all_to_all x2, waiting for transfers between devices, far(): return lax.all_to_all(x.reshape(16, 32, 128), 'far', 0, 0, tiled=True)  9.25 us
  transfers between devices with their start and end apart: 2, of which 2 were waited for; matrix products, arithmetic and copies ran while one was open for 0% of the time, Pallas kernels for 10%

profile of v4, /device:TPU:1, one launch (start us, length us, event | category | flops | bytes accessed | tf_op | source)
XLA Modules:
  0.0 101.2 jit_solution(15427969790441690076)
XLA Ops:
  0.6 1.7 %phase0.1 = f32[16,2,16,128]{3,2,1,0:T(8,128)} custom-call(f32[16,16,128]{2,1,0:T(8,128)} %bitcast.20, f32[16,16,128]{2,1,0:T(8,128)} %bitcast.21), custom_call_target="tpu_custom_call" | custom-call | flops 1048576 | bytes 4194304 | tf_op jit(solution)/shard_map/phase0/pallas_call | solution.py:259
  2.3 18.5 %all-to-all-start = ((f32[16,32,128]{2,1,0:T(8,128)}), f32[16,32,128]{2,1,0:T(8,128)S(1)}, u32[]{:S(2)}, u32[]{:S(2)}) async-start(f32[16,32,128]{2,1,0:T(8,128)} %bitcast.2), calls=%async_computation | async-start | bytes 524288 | tf_op jit(solution)/shard_map/all_to_all | solution.py:282
  20.8 4.9 %prepare_first.1 = (bf16[256,256]{1,0:T(8,128)(2,1)S(1)}, bf16[256,256]{1,0:T(8,128)(2,1)S(1)}, bf16[512,256]{1,0:T(8,128)(2,1)S(1)}, bf16[512,256]{1,0:T(8,128)...) custom-call(f32[3072,128]{1,0:T(8,128)} %bitcast.22, ...), custom_call_target="tpu_custom_call" | custom-call | flops 1258291200 | bytes 4194304 | tf_op jit(solution)/shard_map/prepare_first/pallas_call | solution.py:259
  25.8 4.0 %all-to-all-done = f32[16,32,128]{2,1,0:T(8,128)S(1)} async-done(((f32[16,32,128]{2,1,0:T(8,128)}), f32[16,32,128]{2,1,0:T(8,128)S(1)}, u32[]{:S(2)}, u32[]{:S(2)}) %all-to-all-start) | async-done | bytes 262176 | tf_op jit(solution)/shard_map/all_to_all | solution.py:282
  29.7 1.4 %phase1.1 = f32[512,128]{1,0:T(8,128)S(1)} custom-call(f32[16,2,16,128]{3,2,1,0:T(8,128)S(1)} %bitcast.17, bf16[256,256]{1,0:T(8,128)(2,1)S(1)} %get-tuple-element.22.l01h, bf16[256,256]{1,0:T(8,128)(2,1)S(1)} %get-tuple-element.23.l01l, bf16[512,256]{1,0:T(8,128)(2,1)S(1)} %get-tuple-element.24.w0h, bf16[512,256]{1,0:T(8,128)(2,1)S(1)} %get-tuple-element.25.w0l, ...), custom_call_target="tpu_custom_call" | custom-call | flops 209715200 | bytes 4194304 | tf_op jit(solution)/shard_map/phase1/pallas_call | solution.py:259
  31.1 31.0 %all_to_all.20 = f32[64,8,128]{2,1,0:T(8,128)S(1)} all-to-all(f32[64,8,128]{2,1,0:T(8,128)S(1)} %bitcast.18), channel_id=1, replica_groups=mesh['far'=16,'near'=64] {'near'}, dimensions={0} | all-to-all | bytes 524288 | tf_op jit(solution)/shard_map/all_to_all | solution.py:285
  62.2 1.9 %phase2.1 = f32[16,2,2,8,128]{4,3,2,1,0:T(8,128)} custom-call(f32[512,128]{1,0:T(8,128)S(1)} %bitcast.19, bf16[512,256]{1,0:T(8,128)(2,1)S(1)} %get-tuple-element.28.w12h, bf16[512,256]{1,0:T(8,128)(2,1)S(1)} %get-tuple-element.29.w12l, bf16[512,256]{1,0:T(8,128)(2,1)S(1)} %get-tuple-element.30.w3h, bf16[512,256]{1,0:T(8,128)(2,1)S(1)} %get-tuple-element.31.w3l), custom_call_target="tpu_custom_call" | custom-call | flops 209715200 | bytes 4194304 | tf_op jit(solution)/shard_map/phase2/pallas_call | solution.py:259
  64.1 3.5 %all-to-all-start.2 = ((f32[16,32,128]{2,1,0:T(8,128)}), f32[16,32,128]{2,1,0:T(8,128)S(1)}, u32[]{:S(2)}, u32[]{:S(2)}) async-start(f32[16,32,128]{2,1,0:T(8,128)} %bitcast.8), calls=%async_computation.2 | async-start | bytes 524288 | tf_op jit(solution)/shard_map/all_to_all | solution.py:282
  67.6 5.1 %prepare_second.1 = (bf16[512,256]{1,0:T(8,128)(2,1)S(1)}, bf16[512,256]{1,0:T(8,128)(2,1)S(1)}, bf16[512,256]{1,0:T(8,128)(2,1)S(1)}, bf16[512,256]{1,0:T(8,128...) custom-call(f32[3072,128]{1,0:T(8,128)} %bitcast.23, ...), custom_call_target="tpu_custom_call" | custom-call | flops 1677721600 | bytes 4194304 | tf_op jit(solution)/shard_map/prepare_second/pallas_call | solution.py:259
  72.7 5.3 %all-to-all-done.2 = f32[16,32,128]{2,1,0:T(8,128)S(1)} async-done(((f32[16,32,128]{2,1,0:T(8,128)}), f32[16,32,128]{2,1,0:T(8,128)S(1)}, u32[]{:S(2)}, u32[]{:S(2)}) %all-to-all-start.2) | async-done | bytes 262176 | tf_op jit(solution)/shard_map/all_to_all | solution.py:282
  78.0 1.4 %phase3.1 = f32[512,128]{1,0:T(8,128)S(1)} custom-call(f32[16,2,2,8,128]{4,3,2,1,0:T(8,128)S(1)} %bitcast.14, bf16[512,256]{1,0:T(8,128)(2,1)S(1)} %get-tuple-element.32.w4h, bf16[512,256]{1,0:T(8,128)(2,1)S(1)} %get-tuple-element.33.w4l, bf16[512,256]{1,0:T(8,128)(2,1)S(1)} %get-tuple-element.34.w56h, bf16[512,256]{1,0:T(8,128)(2,1)S(1)} %get-tuple-element.35.w56l, ...), custom_call_target="tpu_custom_call" | custom-call | flops 209715200 | bytes 4194304 | tf_op jit(solution)/shard_map/phase3/pallas_call | solution.py:259
  79.4 20.7 %all_to_all.21 = f32[64,8,128]{2,1,0:T(8,128)S(1)} all-to-all(f32[64,8,128]{2,1,0:T(8,128)S(1)} %bitcast.15), channel_id=1, replica_groups=mesh['far'=16,'near'=64] {'near'}, dimensions={0} | all-to-all | bytes 524288 | tf_op jit(solution)/shard_map/all_to_all | solution.py:285
  100.1 1.1 %phase4.1 = (f32[256,128]{1,0:T(8,128)}, f32[256,128]{1,0:T(8,128)}) custom-call(f32[512,128]{1,0:T(8,128)S(1)} %bitcast.16, bf16[512,256]{1,0:T(8,128)(2,1)S(1)} %get-tuple-element.38.w7h, bf16[512,256]{1,0:T(8,128)(2,1)S(1)} %get-tuple-element.39.w7l), custom_call_target="tpu_custom_call" | custom-call | flops 209715200 | bytes 4194304 | tf_op jit(solution)/shard_map/phase4/pallas_call | solution.py:259
Async XLA Ops:
  2.3 27.4 %all-to-all-start = ((f32[16,32,128]{2,1,0:T(8,128)}), f32[16,32,128]{2,1,0:T(8,128)S(1)}, u32[]{:S(2)}, u32[]{:S(2)}) async-start(f32[16,32,128]{2,1,0:T(8,128)} %bitcast.2), calls=%async_computation | async-start | bytes 524288 | tf_op jit(solution)/shard_map/all_to_all | solution.py:282
  64.1 13.9 %all-to-all-start.2 = ((f32[16,32,128]{2,1,0:T(8,128)}), f32[16,32,128]{2,1,0:T(8,128)S(1)}, u32[]{:S(2)}, u32[]{:S(2)}) async-start(f32[16,32,128]{2,1,0:T(8,128)} %bitcast.8), calls=%async_computation.2 | async-start | bytes 524288 | tf_op jit(solution)/shard_map/all_to_all | solution.py:282

commit v5 on v4

v5 whole, which is shorter than its diff:
```python
import functools

import jax
import jax.numpy as jnp
from jax import lax
from jax.experimental import pallas as pl
from jax.experimental.pallas import tpu as pltpu
from jax.sharding import PartitionSpec as P

F32, BF16 = jnp.float32, jnp.bfloat16
NN = (((1,), (0,)), ((), ()))
NT = (((1,), (1,)), ((), ()))


def split(x):
    hi = x.astype(BF16)
    return hi, (x - hi.astype(F32)).astype(BF16)


def mm(a, b, dims=NN):
    dot = functools.partial(lax.dot_general, dimension_numbers=dims, preferred_element_type=F32)
    return dot(a[0], b[0]) + (dot(a[0], b[1]) + dot(a[1], b[0]))


def cat(parts, axis):
    return jnp.concatenate(parts, axis)


def rows_of(x, n, count):
    return x[n * count : (n + 1) * count]


def merged(r, n):
    k = r.shape[1] // 2
    return r[:n, :k] - r[n:, k:], r[n:, :k] + r[:n, k:]


def big(real, imag):
    return cat([cat([real, -imag], 1), cat([imag, real], 1)], 0)


def lane_bit(shape, stride):
    return (lax.broadcasted_iota(jnp.int32, shape, 1) // stride) % 2 == 0


def swap(a, b, stride):
    even, lanes = lane_bit(a.shape, stride), a.shape[1]
    return (
        jnp.where(even, a, pltpu.roll(b, stride, 1)),
        jnp.where(even, pltpu.roll(a, lanes - stride, 1), b),
    )


def selector(bit):
    i = lax.broadcasted_iota(jnp.int32, (128, 128), 0)
    j = lax.broadcasted_iota(jnp.int32, (128, 128), 1)
    low, top = i % (1 << bit), i // 64
    mid = (i % 64) // (1 << bit)
    return jnp.where(j == mid * (2 << bit) + top * (1 << bit) + low, 1.0, 0.0).astype(BF16)


def columns_moved(x, sel):
    dot = functools.partial(lax.dot_general, dimension_numbers=NT, preferred_element_type=F32)
    hi, lo = split(x)
    return dot(hi, sel) + dot(lo, sel)


def gate(ref, at):
    return ref[pl.ds(at * 128, 128), :]


def odd_even(ref, at):
    return cat([ref[pl.ds(at * 128 + t, 64, 2), :] for t in range(2)], 0)


def both(read, refs, at):
    return cat([read(ref, at) for ref in refs], 0)


def big_of(x):
    n = x.shape[0] // 2
    return tuple(big(a[:n], a[n:]) for a in split(x))


def product(a, b):
    return mm(big_of(a), split(b))


def combined(c, diagonals):
    x = cat([cat([diagonals[t, p] for p in range(2)], 0) for t in range(2)], 1)
    w = mm(big_of(c), split(x))
    return cat([w[p * 128 : (p + 1) * 128, t * 256 : (t + 1) * 256] for p in range(2) for t in range(2)], 0)


def rows_gate(m, c):
    left, diagonals = lane_bit((64, 128), 64), {}
    for p in range(2):
        for t in range(2):
            x = rows_of(m, p * 2 + t, 64)
            y = pltpu.roll(x, 64, 1)
            blocks = [
                cat([jnp.where(left, up, 0.0), jnp.where(left, 0.0, down)], 0)
                for up, down in ((x, y), (y, x))
            ]
            diagonals[t, p] = cat(blocks, 1)
    return combined(c, diagonals)


def put(refs, x):
    refs[0][...], refs[1][...] = split(x)


def prepare(gr, gi, *rest):
    outs, (vr, vi, sems) = [rest[k : k + 2] for k in range(0, 20, 2)], rest[20:]
    l01, m0, c0, l25, w12, w3, w4, w56, l67, w7 = outs
    refs = (vr, vi)
    copies = []
    for s in range(8):
        at = pl.ds(s * 384, 384)
        copies.append(
            [pltpu.make_async_copy(a.at[at], b.at[at], sems.at[s, p]) for p, (a, b) in enumerate(((gr, vr), (gi, vi)))]
        )
        for copy in copies[s]:
            copy.start()

    def ready(s):
        for copy in copies[s]:
            copy.wait()

    sel, second = selector(0), selector(1)
    ready(0)
    put(m0, both(odd_even, refs, 1))
    put(c0, both(gate, refs, 2))
    ready(1)
    put(l01, product(both(gate, refs, 3), both(gate, refs, 0)))
    ready(2)
    moved = columns_moved(
        cat([both(odd_even, refs, 4), both(odd_even, refs, 7), both(gate, refs, 6)], 0), sel
    )
    w1 = rows_gate(rows_of(moved, 0, 256), both(gate, refs, 5))
    w2 = rows_gate(rows_of(moved, 1, 256), both(odd_even, refs, 8))
    put(w12, product(w2, w1))
    ready(3)
    put(w3, rows_gate(columns_moved(both(odd_even, refs, 10), second), both(gate, refs, 11)))
    x = product(both(gate, refs, 9), rows_of(moved, 2, 256))
    ready(4)
    ready(5)
    y = product(both(odd_even, refs, 15), both(gate, refs, 12))
    put(l25, product(y, x))
    ready(6)
    ready(7)
    moved = columns_moved(
        cat([both(odd_even, refs, k) for k in (13, 16, 19, 22)] + [both(gate, refs, 18)], 0), sel
    )
    put(w4, rows_gate(rows_of(moved, 0, 256), both(gate, refs, 14)))
    w5 = rows_gate(rows_of(moved, 1, 256), both(gate, refs, 17))
    w6 = rows_gate(rows_of(moved, 2, 256), both(odd_even, refs, 20))
    put(w56, product(w6, w5))
    put(l67, product(both(gate, refs, 21), rows_of(moved, 4, 256)))
    w = rows_gate(rows_of(moved, 3, 256), both(gate, refs, 23))
    put(w7, cat([columns_moved(w[:, :128], sel), columns_moved(w[:, 128:], sel)], 1))


def read_big(h, l):
    return tuple(big(a[:128], a[128:]) for a in (h[...], l[...]))


def read_blocks(ref):
    return cat(
        [cat([ref[:, p, t].reshape(128, 128) for t in range(2)], 0) for p in range(2)], 1
    )


def read_strided(ref):
    return cat(
        [cat([ref[pl.ds(p * 4 + o, 64, 8), :] for o in range(4)], 0) for p in range(2)], 1
    )


def phase0(sr, si, out, vr, vi, sems):
    pairs = [(sr, vr), (si, vi)]
    copies = [pltpu.make_async_copy(a, b, sems.at[p]) for p, (a, b) in enumerate(pairs)]
    for copy in copies:
        copy.start()
    for p, copy in enumerate(copies):
        copy.wait()
        out[:, p] = pairs[p][1][...]


def phase1(x, l01h, l01l, m0h, m0l, c0h, c0l, l25h, l25l, out):
    y = cat([x[:, p].reshape(256, 128) for p in range(2)], 1)
    y = mm(split(y), read_big(l01h, l01l), NT)
    half = lambda a, k: a[:, k * 128 : (k + 1) * 128]
    y = cat([cat([rows_of(half(y, p), h, 128) for h in range(2)], 1) for p in range(2)], 0)
    y = mm(read_big(m0h, m0l), split(y))
    rows = [cat([half(rows_of(y, 2 * p + t, 64), h) for t in range(2)], 1) for p in range(2) for h in range(2)]
    y = mm(read_big(c0h, c0l), split(cat(rows, 0)))
    o = [rows_of(y, p, 128) for p in range(2)]
    o = [cat([half(a, 0), half(a, 1)], 0) for a in o]
    u = [swap(o[p][:128], o[p][128:], 1) for p in range(2)]
    rows = [u[p][v] for p in range(2) for v in range(2)]
    u = cat([cat([rows_of(r, f, 64) for r in rows], 0) for f in range(2)], 1)
    v = mm(read_big(l25h, l25l), split(u))
    for p in range(2):
        for f in range(2):
            block = v[p * 128 : (p + 1) * 128, f * 128 : (f + 1) * 128]
            for t, y in enumerate(swap(block[:64], block[64:], 1)):
                out[pl.ds(p * 4 + t * 2 + f, 64, 8), :] = y


def phase2(x, w12h, w12l, w3h, w3l, out):
    o = merged(mm((w12h[...], w12l[...]), split(read_strided(x))), 256)
    u = [swap(o[p][:128], o[p][128:], 1) for p in range(2)]
    rows = [u[p][v] for p in range(2) for v in range(2)]
    u = cat([cat([rows_of(r, a, 64) for a in range(2)], 1) for r in rows], 0)
    o = merged(mm((w3h[...], w3l[...]), split(u), NT), 256)
    for p in range(2):
        for t in range(2):
            out[:, p, t] = rows_of(o[p], t, 128).reshape(16, 8, 128)


def phase3(x, w4h, w4l, w56h, w56l, l67h, l67l, out):
    o = merged(mm((w4h[...], w4l[...]), split(read_blocks(x))), 256)
    rows = []
    for p in range(2):
        pairs = [swap(rows_of(o[p], 2 * t, 64), rows_of(o[p], 2 * t + 1, 64), 64) for t in range(2)]
        rows += [cat([pairs[0][v], pairs[1][v]], 1) for v in range(2)]
    o = merged(mm((w56h[...], w56l[...]), split(cat(rows, 0)), NT), 256)
    z = mm(split(cat(o, 1)), read_big(l67h, l67l), NT)
    for p in range(2):
        for k in range(4):
            out[pl.ds(p * 4 + k, 64, 8), :] = z[k * 64 : (k + 1) * 64, p * 128 : (p + 1) * 128]


def phase4(x, w7h, w7l, out_real, out_imag):
    o = merged(mm((w7h[...], w7l[...]), split(read_strided(x))), 256)
    for ref, part in zip((out_real, out_imag), o):
        for t in range(2):
            ref[pl.ds(t, 128, 2), :] = rows_of(part, t, 128)


PARAMS = pltpu.CompilerParams(vmem_limit_bytes=48 << 20)
HILO512 = [jax.ShapeDtypeStruct((512, 256), BF16)] * 2
HILO256 = [jax.ShapeDtypeStruct((256, 128), BF16)] * 2


def call(kernel, name, out_shape, flops, *args, scratch=None, out_specs=None):
    more = {}
    if scratch is not None:
        in_hbm = pl.BlockSpec(memory_space=pltpu.HBM)
        more = {"in_specs": [in_hbm] * len(args), "scratch_shapes": scratch}
    if out_specs is not None:
        more["out_specs"] = out_specs
    return pl.pallas_call(
        kernel,
        out_shape=out_shape,
        compiler_params=PARAMS,
        cost_estimate=pl.CostEstimate(flops=flops, bytes_accessed=4 << 20, transcendentals=0),
        name=name,
        **more,
    )(*args)


def on_device(state_real, state_imag, gate_real, gate_imag):
    shape = state_real.shape
    sr, si, gr, gi = (
        pltpu.with_memory_space_constraint(a, pltpu.HBM)
        for a in (
            state_real.reshape(16, 16, 128), state_imag.reshape(16, 16, 128),
            gate_real.reshape(3072, 128), gate_imag.reshape(3072, 128),
        )
    )
    rows = jax.ShapeDtypeStruct((512, 128), F32)
    blocks = jax.ShapeDtypeStruct((16, 2, 2, 8, 128), F32)

    def far(x):
        return lax.all_to_all(x.reshape(16, 32, 128), "far", 0, 0, tiled=True)

    def near(x):
        x = lax.all_to_all(x.reshape(64, 8, 128), "near", 0, 0, tiled=True)
        return x.reshape(512, 128)

    x = call(
        phase0, "phase0", jax.ShapeDtypeStruct((16, 2, 16, 128), F32), 1 << 20, sr, si,
        scratch=[pltpu.VMEM((16, 16, 128), F32)] * 2 + [pltpu.SemaphoreType.DMA((2,))],
    )
    x = far(x)
    w = call(
        prepare, "prepare",
        HILO256 * 4 + HILO512 * 4 + HILO256 + HILO512, 2400 << 20,
        gr, gi, scratch=[pltpu.VMEM((3072, 128), F32)] * 2 + [pltpu.SemaphoreType.DMA((8, 2))],
    )
    x = near(call(phase1, "phase1", rows, 200 << 20, x.reshape(16, 2, 16, 128), *w[:8]))
    x = far(call(phase2, "phase2", blocks, 200 << 20, x, *w[8:12])).reshape(16, 2, 2, 8, 128)
    x = near(call(phase3, "phase3", rows, 200 << 20, x, *w[12:18]))
    flat = jax.ShapeDtypeStruct((256, 128), F32)
    real, imag = call(phase4, "phase4", [flat, flat], 200 << 20, x, *w[18:])
    return real.reshape(shape), imag.reshape(shape)


def solution(mesh):
    spec = P("far", "near", None, None, None)
    return jax.shard_map(
        on_device,
        mesh=mesh,
        in_specs=(spec, spec, P(), P()),
        out_specs=(spec, spec),
        check_vma=False,
    )
```

time: 102 us -> 101 us (level)
  blocking collectives: 51.7 us -> 66.1 us
  waiting for transfers between devices: 9.25 us -> 1.47 us
  starting transfers between devices: 22 us -> 18.5 us
  Pallas kernels: 17.5 us -> 14.3 us
    all_to_all x0 -> x1, blocking collectives: none -> 12.5 us  [far(): return lax.all_to_all(x.reshape(16, 32, 128), 'far', 0, 0, tiled=True)]
    all_to_all x2 -> x1, waiting for transfers between devices: 9.25 us -> 1.47 us  [far(): return lax.all_to_all(x.reshape(16, 32, 128), 'far', 0, 0, tiled=True)]
    all_to_all x2 -> x1, starting transfers between devices: 22 us -> 18.5 us  [far(): return lax.all_to_all(x.reshape(16, 32, 128), 'far', 0, 0, tiled=True)]
    pallas_call x7 -> x6, Pallas kernels: 17.5 us -> 14.3 us  [call(): pl.pallas_call(kernel, out_shape=out_shape, compiler_params=PARAMS, cost_...]
    all_to_all x2, blocking collectives: 51.7 us -> 53.5 us  [near(): x = lax.all_to_all(x.reshape(64, 8, 128), 'near', 0, 0, tiled=True)]
  transfers between devices with their start and end apart: 2 -> 1, of which waited for: 2 -> 1; matrix products, arithmetic and copies ran while one was open for 0% -> 0% of each run, Pallas kernels for 10% -> 7%
where the time goes in v5:
time: 101 us
  blocking collectives  66.1 us (65%)
  starting transfers between devices  18.5 us (18%)
  Pallas kernels  14.3 us (14%)
  waiting for transfers between devices  1.47 us (1%)
    all_to_all x2, blocking collectives, near(): x = lax.all_to_all(x.reshape(64, 8, 128), 'near', 0, 0, tiled=True)  53.5 us
    all_to_all x1, starting transfers between devices, far(): return lax.all_to_all(x.reshape(16, 32, 128), 'far', 0, 0, tiled=True)  18.5 us
    pallas_call x6, Pallas kernels, call(): pl.pallas_call(kernel, out_shape=out_shape, compiler_params=PARAMS, cost_...  14.3 us
    all_to_all x1, blocking collectives, far(): return lax.all_to_all(x.reshape(16, 32, 128), 'far', 0, 0, tiled=True)  12.5 us
  transfers between devices with their start and end apart: 1, of which 1 were waited for; matrix products, arithmetic and copies ran while one was open for 0% of the time, Pallas kernels for 7%

profile of v5, /device:TPU:1, one launch (start us, length us, event | category | flops | bytes accessed | tf_op | source)
XLA Modules:
  0.0 101.0 jit_solution(14085970541628652394)
XLA Ops:
  0.6 1.7 %phase0.1 = f32[16,2,16,128]{3,2,1,0:T(8,128)} custom-call(f32[16,16,128]{2,1,0:T(8,128)} %bitcast.21, f32[16,16,128]{2,1,0:T(8,128)} %bitcast.22), custom_call_target="tpu_custom_call" | custom-call | flops 1048576 | bytes 4194304 | tf_op jit(solution)/shard_map/phase0/pallas_call | solution.py:254
  2.3 18.5 %all-to-all-start = ((f32[16,32,128]{2,1,0:T(8,128)}), f32[16,32,128]{2,1,0:T(8,128)S(1)}, u32[]{:S(2)}, u32[]{:S(2)}) async-start(f32[16,32,128]{2,1,0:T(8,128)} %bitcast.2), calls=%async_computation | async-start | bytes 524288 | tf_op jit(solution)/shard_map/all_to_all | solution.py:277
  20.8 7.5 %prepare.1 = (bf16[256,128]{1,0:T(8,128)(2,1)S(1)}, bf16[256,128]{1,0:T(8,128)(2,1)S(1)}, bf16[256,128]{1,0:T(8,128)(2,1)S(1)}, bf16[256,128]{1,0:T(8,128)(2,1)S...) custom-call(f32[3072,128]{1,0:T(8,128)} %bitcast.23, ...), custom_call_target="tpu_custom_call" | custom-call | flops 2516582400 | bytes 4194304 | tf_op jit(solution)/shard_map/prepare/pallas_call | solution.py:254
  28.3 1.5 %all-to-all-done = f32[16,32,128]{2,1,0:T(8,128)S(1)} async-done(((f32[16,32,128]{2,1,0:T(8,128)}), f32[16,32,128]{2,1,0:T(8,128)S(1)}, u32[]{:S(2)}, u32[]{:S(2)}) %all-to-all-start) | async-done | bytes 262176 | tf_op jit(solution)/shard_map/all_to_all | solution.py:277
  29.7 1.5 %phase1.1 = f32[512,128]{1,0:T(8,128)S(1)} custom-call(f32[16,2,16,128]{3,2,1,0:T(8,128)S(1)} %bitcast.15, bf16[256,128]{1,0:T(8,128)(2,1)S(1)} %get-tuple-element.24.l01h, bf16[256,128]{1,0:T(8,128)(2,1)S(1)} %get-tuple-element.25.l01l, bf16[256,128]{1,0:T(8,128)(2,1)S(1)} %get-tuple-element.26.m0h, bf16[256,128]{1,0:T(8,128)(2,1)S(1)} %get-tuple-element.27.m0l, ...), custom_call_target="tpu_custom_call" | custom-call | flops 209715200 | bytes 4194304 | tf_op jit(solution)/shard_map/phase1/pallas_call | solution.py:254
  31.2 31.0 %all_to_all.20 = f32[64,8,128]{2,1,0:T(8,128)S(1)} all-to-all(f32[64,8,128]{2,1,0:T(8,128)S(1)} %bitcast.16), channel_id=1, replica_groups=mesh['far'=16,'near'=64] {'near'}, dimensions={0} | all-to-all | bytes 524288 | tf_op jit(solution)/shard_map/all_to_all | solution.py:280
  62.3 1.2 %phase2.1 = f32[16,2,2,8,128]{4,3,2,1,0:T(8,128)S(1)} custom-call(f32[512,128]{1,0:T(8,128)S(1)} %bitcast.19, bf16[512,256]{1,0:T(8,128)(2,1)S(1)} %get-tuple-element.32.w12h, bf16[512,256]{1,0:T(8,128)(2,1)S(1)} %get-tuple-element.33.w12l, bf16[512,256]{1,0:T(8,128)(2,1)S(1)} %get-tuple-element.34.w3h, bf16[512,256]{1,0:T(8,128)(2,1)S(1)} %get-tuple-element.35.w3l), custom_call_target="tpu_custom_call" | custom-call | flops 209715200 | bytes 4194304 | tf_op jit(solution)/shard_map/phase2/pallas_call | solution.py:254
  63.5 12.5 %all_to_all.21 = f32[16,32,128]{2,1,0:T(8,128)S(1)} all-to-all(f32[16,32,128]{2,1,0:T(8,128)S(1)} %bitcast.20), channel_id=1, replica_groups=mesh['far'=16,'near'=64] {'far'}, dimensions={0} | all-to-all | bytes 524288 | tf_op jit(solution)/shard_map/all_to_all | solution.py:277
  76.0 1.4 %phase3.1 = f32[512,128]{1,0:T(8,128)S(1)} custom-call(f32[16,2,2,8,128]{4,3,2,1,0:T(8,128)S(1)} %bitcast.17, bf16[512,256]{1,0:T(8,128)(2,1)S(1)} %get-tuple-element.36.w4h, bf16[512,256]{1,0:T(8,128)(2,1)S(1)} %get-tuple-element.37.w4l, bf16[512,256]{1,0:T(8,128)(2,1)S(1)} %get-tuple-element.38.w56h, bf16[512,256]{1,0:T(8,128)(2,1)S(1)} %get-tuple-element.39.w56l, ...), custom_call_target="tpu_custom_call" | custom-call | flops 209715200 | bytes 4194304 | tf_op jit(solution)/shard_map/phase3/pallas_call | solution.py:254
  77.4 22.5 %all_to_all.22 = f32[64,8,128]{2,1,0:T(8,128)S(1)} all-to-all(f32[64,8,128]{2,1,0:T(8,128)S(1)} %bitcast.18), channel_id=1, replica_groups=mesh['far'=16,'near'=64] {'near'}, dimensions={0} | all-to-all | bytes 524288 | tf_op jit(solution)/shard_map/all_to_all | solution.py:280
  99.9 1.1 %phase4.1 = (f32[256,128]{1,0:T(8,128)}, f32[256,128]{1,0:T(8,128)}) custom-call(f32[512,128]{1,0:T(8,128)S(1)} %bitcast.14, bf16[512,256]{1,0:T(8,128)(2,1)S(1)} %get-tuple-element.42.w7h, bf16[512,256]{1,0:T(8,128)(2,1)S(1)} %get-tuple-element.43.w7l), custom_call_target="tpu_custom_call" | custom-call | flops 209715200 | bytes 4194304 | tf_op jit(solution)/shard_map/phase4/pallas_call | solution.py:254
Async XLA Ops:
  2.3 27.4 %all-to-all-start = ((f32[16,32,128]{2,1,0:T(8,128)}), f32[16,32,128]{2,1,0:T(8,128)S(1)}, u32[]{:S(2)}, u32[]{:S(2)}) async-start(f32[16,32,128]{2,1,0:T(8,128)} %bitcast.2), calls=%async_computation | async-start | bytes 524288 | tf_op jit(solution)/shard_map/all_to_all | solution.py:277

commit v6 on v5

--- a/solution.py
+++ b/solution.py
@@ -22,6 +22,11 @@
     return dot(a[0], b[0]) + (dot(a[0], b[1]) + dot(a[1], b[0]))
 
 
+def mm_rows(a, b, dims=NN, step=128):
+    n = a[0].shape[0]
+    return cat([mm(tuple(p[k : k + step] for p in a), b, dims) for k in range(0, n, step)], 0)
+
+
 def cat(parts, axis):
     return jnp.concatenate(parts, axis)
 
@@ -33,6 +38,14 @@
 def merged(r, n):
     k = r.shape[1] // 2
     return r[:n, :k] - r[n:, k:], r[n:, :k] + r[:n, k:]
+
+
+def applied(h, l, x, dims=NN):
+    parts = []
+    for k in range(0, 256, 128):
+        w = tuple(cat([ref[pl.ds(k, 128), :], ref[pl.ds(256 + k, 128), :]], 0) for ref in (h, l))
+        parts.append(merged(mm(w, x, dims), 128))
+    return tuple(cat([p[k] for p in parts], 0) for k in range(2))
 
 
 def big(real, imag):
@@ -83,12 +96,12 @@
 
 
 def product(a, b):
-    return mm(big_of(a), split(b))
+    return mm_rows(big_of(a), split(b))
 
 
 def combined(c, diagonals):
     x = cat([cat([diagonals[t, p] for p in range(2)], 0) for t in range(2)], 1)
-    w = mm(big_of(c), split(x))
+    w = mm_rows(big_of(c), split(x))
     return cat([w[p * 128 : (p + 1) * 128, t * 256 : (t + 1) * 256] for p in range(2) for t in range(2)], 0)
 
 
@@ -189,18 +202,18 @@
 
 def phase1(x, l01h, l01l, m0h, m0l, c0h, c0l, l25h, l25l, out):
     y = cat([x[:, p].reshape(256, 128) for p in range(2)], 1)
-    y = mm(split(y), read_big(l01h, l01l), NT)
+    y = mm_rows(split(y), read_big(l01h, l01l), NT)
     half = lambda a, k: a[:, k * 128 : (k + 1) * 128]
     y = cat([cat([rows_of(half(y, p), h, 128) for h in range(2)], 1) for p in range(2)], 0)
-    y = mm(read_big(m0h, m0l), split(y))
+    y = mm_rows(read_big(m0h, m0l), split(y))
     rows = [cat([half(rows_of(y, 2 * p + t, 64), h) for t in range(2)], 1) for p in range(2) for h in range(2)]
-    y = mm(read_big(c0h, c0l), split(cat(rows, 0)))
+    y = mm_rows(read_big(c0h, c0l), split(cat(rows, 0)))
     o = [rows_of(y, p, 128) for p in range(2)]
     o = [cat([half(a, 0), half(a, 1)], 0) for a in o]
     u = [swap(o[p][:128], o[p][128:], 1) for p in range(2)]
     rows = [u[p][v] for p in range(2) for v in range(2)]
     u = cat([cat([rows_of(r, f, 64) for r in rows], 0) for f in range(2)], 1)
-    v = mm(read_big(l25h, l25l), split(u))
+    v = mm_rows(read_big(l25h, l25l), split(u))
     for p in range(2):
         for f in range(2):
             block = v[p * 128 : (p + 1) * 128, f * 128 : (f + 1) * 128]
@@ -209,31 +222,31 @@
 
 
 def phase2(x, w12h, w12l, w3h, w3l, out):
-    o = merged(mm((w12h[...], w12l[...]), split(read_strided(x))), 256)
+    o = applied(w12h, w12l, split(read_strided(x)))
     u = [swap(o[p][:128], o[p][128:], 1) for p in range(2)]
     rows = [u[p][v] for p in range(2) for v in range(2)]
     u = cat([cat([rows_of(r, a, 64) for a in range(2)], 1) for r in rows], 0)
-    o = merged(mm((w3h[...], w3l[...]), split(u), NT), 256)
+    o = applied(w3h, w3l, split(u), NT)
     for p in range(2):
         for t in range(2):
             out[:, p, t] = rows_of(o[p], t, 128).reshape(16, 8, 128)
 
 
 def phase3(x, w4h, w4l, w56h, w56l, l67h, l67l, out):
-    o = merged(mm((w4h[...], w4l[...]), split(read_blocks(x))), 256)
+    o = applied(w4h, w4l, split(read_blocks(x)))
     rows = []
     for p in range(2):
         pairs = [swap(rows_of(o[p], 2 * t, 64), rows_of(o[p], 2 * t + 1, 64), 64) for t in range(2)]
         rows += [cat([pairs[0][v], pairs[1][v]], 1) for v in range(2)]
-    o = merged(mm((w56h[...], w56l[...]), split(cat(rows, 0)), NT), 256)
-    z = mm(split(cat(o, 1)), read_big(l67h, l67l), NT)
+    o = applied(w56h, w56l, split(cat(rows, 0)), NT)
+    z = mm_rows(split(cat(o, 1)), read_big(l67h, l67l), NT)
     for p in range(2):
         for k in range(4):
             out[pl.ds(p * 4 + k, 64, 8), :] = z[k * 64 : (k + 1) * 64, p * 128 : (p + 1) * 128]
 
 
 def phase4(x, w7h, w7l, out_real, out_imag):
-    o = merged(mm((w7h[...], w7l[...]), split(read_strided(x))), 256)
+    o = applied(w7h, w7l, split(read_strided(x)))
     for ref, part in zip((out_real, out_imag), o):
         for t in range(2):
             ref[pl.ds(t, 128, 2), :] = rows_of(part, t, 128)

time: 101 us -> 100 us (0.990)
  Pallas kernels: 14.3 us -> 13 us
    pallas_call x6, Pallas kernels: 14.3 us -> 13 us  [call(): pl.pallas_call(kernel, out_shape=out_shape, compiler_params=PARAMS, cost_...]
where the time goes in v6:
time: 100 us; the launch traced here: 99.6 us
  blocking collectives  65.5 us (66%)
  starting transfers between devices  18.5 us (18%)
  Pallas kernels  13 us (13%)
  waiting for transfers between devices  2.06 us (2%)
    all_to_all x2, blocking collectives, near(): x = lax.all_to_all(x.reshape(64, 8, 128), 'near', 0, 0, tiled=True)  53.5 us
    all_to_all x1, starting transfers between devices, far(): return lax.all_to_all(x.reshape(16, 32, 128), 'far', 0, 0, tiled=True)  18.5 us
    pallas_call x6, Pallas kernels, call(): pl.pallas_call(kernel, out_shape=out_shape, compiler_params=PARAMS, cost_...  13 us
    all_to_all x1, blocking collectives, far(): return lax.all_to_all(x.reshape(16, 32, 128), 'far', 0, 0, tiled=True)  11.9 us
    all_to_all x1, waiting for transfers between devices, far(): return lax.all_to_all(x.reshape(16, 32, 128), 'far', 0, 0, tiled=True)  2.06 us
  transfers between devices with their start and end apart: 1, of which 1 were waited for; matrix products, arithmetic and copies ran while one was open for 0% of the time, Pallas kernels for 7%

profile of v6, /device:TPU:1, one launch (start us, length us, event | category | flops | bytes accessed | tf_op | source)
XLA Modules:
  0.0 99.6 jit_solution(16519449285179450731)
XLA Ops:
  0.6 1.7 %phase0.1 = f32[16,2,16,128]{3,2,1,0:T(8,128)} custom-call(f32[16,16,128]{2,1,0:T(8,128)} %bitcast.21, f32[16,16,128]{2,1,0:T(8,128)} %bitcast.22), custom_call_target="tpu_custom_call" | custom-call | flops 1048576 | bytes 4194304 | tf_op jit(solution)/shard_map/phase0/pallas_call | solution.py:267
  2.3 18.5 %all-to-all-start = ((f32[16,32,128]{2,1,0:T(8,128)}), f32[16,32,128]{2,1,0:T(8,128)S(1)}, u32[]{:S(2)}, u32[]{:S(2)}) async-start(f32[16,32,128]{2,1,0:T(8,128)} %bitcast.2), calls=%async_computation | async-start | bytes 524288 | tf_op jit(solution)/shard_map/all_to_all | solution.py:290
  20.8 6.9 %prepare.1 = (bf16[256,128]{1,0:T(8,128)(2,1)S(1)}, bf16[256,128]{1,0:T(8,128)(2,1)S(1)}, bf16[256,128]{1,0:T(8,128)(2,1)S(1)}, bf16[256,128]{1,0:T(8,128)(2,1)S...) custom-call(f32[3072,128]{1,0:T(8,128)} %bitcast.23, ...), custom_call_target="tpu_custom_call" | custom-call | flops 2516582400 | bytes 4194304 | tf_op jit(solution)/shard_map/prepare/pallas_call | solution.py:267
  27.7 2.1 %all-to-all-done = f32[16,32,128]{2,1,0:T(8,128)S(1)} async-done(((f32[16,32,128]{2,1,0:T(8,128)}), f32[16,32,128]{2,1,0:T(8,128)S(1)}, u32[]{:S(2)}, u32[]{:S(2)}) %all-to-all-start) | async-done | bytes 262176 | tf_op jit(solution)/shard_map/all_to_all | solution.py:290
  29.7 1.4 %phase1.1 = f32[512,128]{1,0:T(8,128)S(1)} custom-call(f32[16,2,16,128]{3,2,1,0:T(8,128)S(1)} %bitcast.15, bf16[256,128]{1,0:T(8,128)(2,1)S(1)} %get-tuple-element.24.l01h, bf16[256,128]{1,0:T(8,128)(2,1)S(1)} %get-tuple-element.25.l01l, bf16[256,128]{1,0:T(8,128)(2,1)S(1)} %get-tuple-element.26.m0h, bf16[256,128]{1,0:T(8,128)(2,1)S(1)} %get-tuple-element.27.m0l, ...), custom_call_target="tpu_custom_call" | custom-call | flops 209715200 | bytes 4194304 | tf_op jit(solution)/shard_map/phase1/pallas_call | solution.py:267
  31.1 31.0 %all_to_all.20 = f32[64,8,128]{2,1,0:T(8,128)S(1)} all-to-all(f32[64,8,128]{2,1,0:T(8,128)S(1)} %bitcast.16), channel_id=1, replica_groups=mesh['far'=16,'near'=64] {'near'}, dimensions={0} | all-to-all | bytes 524288 | tf_op jit(solution)/shard_map/all_to_all | solution.py:293
  62.2 0.8 phase2.1
  63.0 11.9 %all_to_all.21 = f32[16,32,128]{2,1,0:T(8,128)S(1)} all-to-all(f32[16,32,128]{2,1,0:T(8,128)S(1)} %bitcast.20), channel_id=1, replica_groups=mesh['far'=16,'near'=64] {'far'}, dimensions={0} | all-to-all | bytes 524288 | tf_op jit(solution)/shard_map/all_to_all | solution.py:290
  74.9 1.1 %phase3.1 = f32[512,128]{1,0:T(8,128)S(1)} custom-call(f32[16,2,2,8,128]{4,3,2,1,0:T(8,128)S(1)} %bitcast.17, bf16[512,256]{1,0:T(8,128)(2,1)S(1)} %get-tuple-element.36.w4h, bf16[512,256]{1,0:T(8,128)(2,1)S(1)} %get-tuple-element.37.w4l, bf16[512,256]{1,0:T(8,128)(2,1)S(1)} %get-tuple-element.38.w56h, bf16[512,256]{1,0:T(8,128)(2,1)S(1)} %get-tuple-element.39.w56l, ...), custom_call_target="tpu_custom_call" | custom-call | flops 209715200 | bytes 4194304 | tf_op jit(solution)/shard_map/phase3/pallas_call | solution.py:267
  76.1 22.5 %all_to_all.22 = f32[64,8,128]{2,1,0:T(8,128)S(1)} all-to-all(f32[64,8,128]{2,1,0:T(8,128)S(1)} %bitcast.18), channel_id=1, replica_groups=mesh['far'=16,'near'=64] {'near'}, dimensions={0} | all-to-all | bytes 524288 | tf_op jit(solution)/shard_map/all_to_all | solution.py:293
  98.6 1.1 %phase4.1 = (f32[256,128]{1,0:T(8,128)}, f32[256,128]{1,0:T(8,128)}) custom-call(f32[512,128]{1,0:T(8,128)S(1)} %bitcast.14, bf16[512,256]{1,0:T(8,128)(2,1)S(1)} %get-tuple-element.42.w7h, bf16[512,256]{1,0:T(8,128)(2,1)S(1)} %get-tuple-element.43.w7l), custom_call_target="tpu_custom_call" | custom-call | flops 209715200 | bytes 4194304 | tf_op jit(solution)/shard_map/phase4/pallas_call | solution.py:267
Async XLA Ops:
  2.3 27.4 %all-to-all-start = ((f32[16,32,128]{2,1,0:T(8,128)}), f32[16,32,128]{2,1,0:T(8,128)S(1)}, u32[]{:S(2)}, u32[]{:S(2)}) async-start(f32[16,32,128]{2,1,0:T(8,128)} %bitcast.2), calls=%async_computation | async-start | bytes 524288 | tf_op jit(solution)/shard_map/all_to_all | solution.py:290

commit v7 on v6

--- a/solution.py
+++ b/solution.py
@@ -145,7 +145,7 @@
     put(m0, both(odd_even, refs, 1))
     put(c0, both(gate, refs, 2))
     ready(1)
-    put(l01, product(both(gate, refs, 3), both(gate, refs, 0)))
+    put(l01, turned(product(both(gate, refs, 3), both(gate, refs, 0))))
     ready(2)
     moved = columns_moved(
         cat([both(odd_even, refs, 4), both(odd_even, refs, 7), both(gate, refs, 6)], 0), sel
@@ -169,9 +169,18 @@
     w5 = rows_gate(rows_of(moved, 1, 256), both(gate, refs, 17))
     w6 = rows_gate(rows_of(moved, 2, 256), both(odd_even, refs, 20))
     put(w56, product(w6, w5))
-    put(l67, product(both(gate, refs, 21), rows_of(moved, 4, 256)))
+    put(l67, turned(product(both(gate, refs, 21), rows_of(moved, 4, 256))))
     w = rows_gate(rows_of(moved, 3, 256), both(gate, refs, 23))
     put(w7, cat([columns_moved(w[:, :128], sel), columns_moved(w[:, 128:], sel)], 1))
+
+
+def turned(x):
+    n = x.shape[0] // 2
+    return cat([x[:n].T, x[n:].T], 0)
+
+
+def read_turned(h, l):
+    return tuple(big(a[:128], -a[128:]) for a in (h[...], l[...]))
 
 
 def read_big(h, l):
@@ -202,7 +211,7 @@
 
 def phase1(x, l01h, l01l, m0h, m0l, c0h, c0l, l25h, l25l, out):
     y = cat([x[:, p].reshape(256, 128) for p in range(2)], 1)
-    y = mm_rows(split(y), read_big(l01h, l01l), NT)
+    y = mm_rows(split(y), read_turned(l01h, l01l))
     half = lambda a, k: a[:, k * 128 : (k + 1) * 128]
     y = cat([cat([rows_of(half(y, p), h, 128) for h in range(2)], 1) for p in range(2)], 0)
     y = mm_rows(read_big(m0h, m0l), split(y))
@@ -239,7 +248,7 @@
         pairs = [swap(rows_of(o[p], 2 * t, 64), rows_of(o[p], 2 * t + 1, 64), 64) for t in range(2)]
         rows += [cat([pairs[0][v], pairs[1][v]], 1) for v in range(2)]
     o = applied(w56h, w56l, split(cat(rows, 0)), NT)
-    z = mm_rows(split(cat(o, 1)), read_big(l67h, l67l), NT)
+    z = mm_rows(split(cat(o, 1)), read_turned(l67h, l67l))
     for p in range(2):
         for k in range(4):
             out[pl.ds(p * 4 + k, 64, 8), :] = z[k * 64 : (k + 1) * 64, p * 128 : (p + 1) * 128]

time: 100 us -> 99.9 us (level)
  no operation moved by 1% of the time
where the time goes in v7:
time: 99.9 us; the launch traced here: 99.5 us
  blocking collectives  65.5 us (66%)
  starting transfers between devices  18.5 us (19%)
  Pallas kernels  12.8 us (13%)
  waiting for transfers between devices  1.98 us (2%)
    all_to_all x2, blocking collectives, near(): x = lax.all_to_all(x.reshape(64, 8, 128), 'near', 0, 0, tiled=True)  53.5 us
    all_to_all x1, starting transfers between devices, far(): return lax.all_to_all(x.reshape(16, 32, 128), 'far', 0, 0, tiled=True)  18.5 us
    pallas_call x6, Pallas kernels, call(): pl.pallas_call(kernel, out_shape=out_shape, compiler_params=PARAMS, cost_...  12.8 us
    all_to_all x1, blocking collectives, far(): return lax.all_to_all(x.reshape(16, 32, 128), 'far', 0, 0, tiled=True)  12 us
  transfers between devices with their start and end apart: 1, of which 1 were waited for; matrix products, arithmetic and copies ran while one was open for 0% of the time, Pallas kernels for 7%

profile of v7, /device:TPU:1, one launch (start us, length us, event | category | flops | bytes accessed | tf_op | source)
XLA Modules:
  0.0 99.5 jit_solution(16938187807009561585)
XLA Ops:
  0.6 1.7 %phase0.1 = f32[16,2,16,128]{3,2,1,0:T(8,128)} custom-call(f32[16,16,128]{2,1,0:T(8,128)} %bitcast.21, f32[16,16,128]{2,1,0:T(8,128)} %bitcast.22), custom_call_target="tpu_custom_call" | custom-call | flops 1048576 | bytes 4194304 | tf_op jit(solution)/shard_map/phase0/pallas_call | solution.py:276
  2.3 18.5 %all-to-all-start = ((f32[16,32,128]{2,1,0:T(8,128)}), f32[16,32,128]{2,1,0:T(8,128)S(1)}, u32[]{:S(2)}, u32[]{:S(2)}) async-start(f32[16,32,128]{2,1,0:T(8,128)} %bitcast.2), calls=%async_computation | async-start | bytes 524288 | tf_op jit(solution)/shard_map/all_to_all | solution.py:299
  20.8 6.9 %prepare.1 = (bf16[256,128]{1,0:T(8,128)(2,1)S(1)}, bf16[256,128]{1,0:T(8,128)(2,1)S(1)}, bf16[256,128]{1,0:T(8,128)(2,1)S(1)}, bf16[256,128]{1,0:T(8,128)(2,1)S...) custom-call(f32[3072,128]{1,0:T(8,128)} %bitcast.23, ...), custom_call_target="tpu_custom_call" | custom-call | flops 2516582400 | bytes 4194304 | tf_op jit(solution)/shard_map/prepare/pallas_call | solution.py:276
  27.7 2.0 %all-to-all-done = f32[16,32,128]{2,1,0:T(8,128)S(1)} async-done(((f32[16,32,128]{2,1,0:T(8,128)}), f32[16,32,128]{2,1,0:T(8,128)S(1)}, u32[]{:S(2)}, u32[]{:S(2)}) %all-to-all-start) | async-done | bytes 262176 | tf_op jit(solution)/shard_map/all_to_all | solution.py:299
  29.7 1.3 %phase1.1 = f32[512,128]{1,0:T(8,128)S(1)} custom-call(f32[16,2,16,128]{3,2,1,0:T(8,128)S(1)} %bitcast.15, bf16[256,128]{1,0:T(8,128)(2,1)S(1)} %get-tuple-element.24.l01h, bf16[256,128]{1,0:T(8,128)(2,1)S(1)} %get-tuple-element.25.l01l, bf16[256,128]{1,0:T(8,128)(2,1)S(1)} %get-tuple-element.26.m0h, bf16[256,128]{1,0:T(8,128)(2,1)S(1)} %get-tuple-element.27.m0l, ...), custom_call_target="tpu_custom_call" | custom-call | flops 209715200 | bytes 4194304 | tf_op jit(solution)/shard_map/phase1/pallas_call | solution.py:276
  31.0 31.0 %all_to_all.20 = f32[64,8,128]{2,1,0:T(8,128)S(1)} all-to-all(f32[64,8,128]{2,1,0:T(8,128)S(1)} %bitcast.16), channel_id=1, replica_groups=mesh['far'=16,'near'=64] {'near'}, dimensions={0} | all-to-all | bytes 524288 | tf_op jit(solution)/shard_map/all_to_all | solution.py:302
  62.0 0.8 phase2.1
  62.9 12.0 %all_to_all.21 = f32[16,32,128]{2,1,0:T(8,128)S(1)} all-to-all(f32[16,32,128]{2,1,0:T(8,128)S(1)} %bitcast.20), channel_id=1, replica_groups=mesh['far'=16,'near'=64] {'far'}, dimensions={0} | all-to-all | bytes 524288 | tf_op jit(solution)/shard_map/all_to_all | solution.py:299
  74.9 1.1 %phase3.1 = f32[512,128]{1,0:T(8,128)S(1)} custom-call(f32[16,2,2,8,128]{4,3,2,1,0:T(8,128)S(1)} %bitcast.17, bf16[512,256]{1,0:T(8,128)(2,1)S(1)} %get-tuple-element.36.w4h, bf16[512,256]{1,0:T(8,128)(2,1)S(1)} %get-tuple-element.37.w4l, bf16[512,256]{1,0:T(8,128)(2,1)S(1)} %get-tuple-element.38.w56h, bf16[512,256]{1,0:T(8,128)(2,1)S(1)} %get-tuple-element.39.w56l, ...), custom_call_target="tpu_custom_call" | custom-call | flops 209715200 | bytes 4194304 | tf_op jit(solution)/shard_map/phase3/pallas_call | solution.py:276
  76.0 22.5 %all_to_all.22 = f32[64,8,128]{2,1,0:T(8,128)S(1)} all-to-all(f32[64,8,128]{2,1,0:T(8,128)S(1)} %bitcast.18), channel_id=1, replica_groups=mesh['far'=16,'near'=64] {'near'}, dimensions={0} | all-to-all | bytes 524288 | tf_op jit(solution)/shard_map/all_to_all | solution.py:302
  98.4 1.1 %phase4.1 = (f32[256,128]{1,0:T(8,128)}, f32[256,128]{1,0:T(8,128)}) custom-call(f32[512,128]{1,0:T(8,128)S(1)} %bitcast.14, bf16[512,256]{1,0:T(8,128)(2,1)S(1)} %get-tuple-element.42.w7h, bf16[512,256]{1,0:T(8,128)(2,1)S(1)} %get-tuple-element.43.w7l), custom_call_target="tpu_custom_call" | custom-call | flops 209715200 | bytes 4194304 | tf_op jit(solution)/shard_map/phase4/pallas_call | solution.py:276
Async XLA Ops:
  2.3 27.4 %all-to-all-start = ((f32[16,32,128]{2,1,0:T(8,128)}), f32[16,32,128]{2,1,0:T(8,128)S(1)}, u32[]{:S(2)}, u32[]{:S(2)}) async-start(f32[16,32,128]{2,1,0:T(8,128)} %bitcast.2), calls=%async_computation | async-start | bytes 524288 | tf_op jit(solution)/shard_map/all_to_all | solution.py:299

commit v8 on v7

--- a/solution.py
+++ b/solution.py
@@ -199,14 +199,22 @@
     )
 
 
-def phase0(sr, si, out, vr, vi, sems):
-    pairs = [(sr, vr), (si, vi)]
-    copies = [pltpu.make_async_copy(a, b, sems.at[p]) for p, (a, b) in enumerate(pairs)]
-    for copy in copies:
-        copy.start()
-    for p, copy in enumerate(copies):
-        copy.wait()
-        out[:, p] = pairs[p][1][...]
+def phase0(sr, si, out, vr, vi, vm, sems):
+    fetches, sends = [], []
+    for k in range(4):
+        at = pl.ds(k * 4, 4)
+        for p, (a, b) in enumerate(((sr, vr), (si, vi))):
+            fetches.append(pltpu.make_async_copy(a.at[at], b.at[at], sems.at[p, k]))
+            fetches[-1].start()
+    for k in range(4):
+        at = pl.ds(k * 4, 4)
+        for p, b in enumerate((vr, vi)):
+            fetches[2 * k + p].wait()
+            vm[at, p] = b[at]
+        sends.append(pltpu.make_async_copy(vm.at[at], out.at[at], sems.at[2, k]))
+        sends[-1].start()
+    for send in sends:
+        send.wait()
 
 
 def phase1(x, l01h, l01l, m0h, m0l, c0h, c0l, l25h, l25l, out):
@@ -304,7 +312,9 @@
 
     x = call(
         phase0, "phase0", jax.ShapeDtypeStruct((16, 2, 16, 128), F32), 1 << 20, sr, si,
-        scratch=[pltpu.VMEM((16, 16, 128), F32)] * 2 + [pltpu.SemaphoreType.DMA((2,))],
+        scratch=[pltpu.VMEM((16, 16, 128), F32)] * 2
+        + [pltpu.VMEM((16, 2, 16, 128), F32), pltpu.SemaphoreType.DMA((3, 4))],
+        out_specs=pl.BlockSpec(memory_space=pltpu.HBM),
     )
     x = far(x)
     w = call(

time: 99.9 us -> 99.8 us (level)
  no operation moved by 1% of the time
where the time goes in v8:
time: 99.8 us; the launch traced here: 99.4 us
  blocking collectives  65.6 us (66%)
  starting transfers between devices  18.5 us (19%)
  Pallas kernels  12.8 us (13%)
  waiting for transfers between devices  1.98 us (2%)
    all_to_all x2, blocking collectives, near(): x = lax.all_to_all(x.reshape(64, 8, 128), 'near', 0, 0, tiled=True)  53.5 us
    all_to_all x1, starting transfers between devices, far(): return lax.all_to_all(x.reshape(16, 32, 128), 'far', 0, 0, tiled=True)  18.5 us
    pallas_call x6, Pallas kernels, call(): pl.pallas_call(kernel, out_shape=out_shape, compiler_params=PARAMS, cost_...  12.8 us
    all_to_all x1, blocking collectives, far(): return lax.all_to_all(x.reshape(16, 32, 128), 'far', 0, 0, tiled=True)  12 us
  transfers between devices with their start and end apart: 1, of which 1 were waited for; matrix products, arithmetic and copies ran while one was open for 0% of the time, Pallas kernels for 7%

profile of v8, /device:TPU:1, one launch (start us, length us, event | category | flops | bytes accessed | tf_op | source)
XLA Modules:
  0.0 99.4 jit_solution(2659060007264109816)
XLA Ops:
  0.6 1.6 %phase0.1 = f32[16,2,16,128]{3,2,1,0:T(8,128)} custom-call(f32[16,16,128]{2,1,0:T(8,128)} %bitcast.21, f32[16,16,128]{2,1,0:T(8,128)} %bitcast.22), custom_call_target="tpu_custom_call" | custom-call | flops 1048576 | bytes 4194304 | tf_op jit(solution)/shard_map/phase0/pallas_call | solution.py:284
  2.2 18.5 %all-to-all-start = ((f32[16,32,128]{2,1,0:T(8,128)}), f32[16,32,128]{2,1,0:T(8,128)S(1)}, u32[]{:S(2)}, u32[]{:S(2)}) async-start(f32[16,32,128]{2,1,0:T(8,128)} %bitcast.2), calls=%async_computation | async-start | bytes 524288 | tf_op jit(solution)/shard_map/all_to_all | solution.py:307
  20.7 6.9 %prepare.1 = (bf16[256,128]{1,0:T(8,128)(2,1)S(1)}, bf16[256,128]{1,0:T(8,128)(2,1)S(1)}, bf16[256,128]{1,0:T(8,128)(2,1)S(1)}, bf16[256,128]{1,0:T(8,128)(2,1)S...) custom-call(f32[3072,128]{1,0:T(8,128)} %bitcast.23, ...), custom_call_target="tpu_custom_call" | custom-call | flops 2516582400 | bytes 4194304 | tf_op jit(solution)/shard_map/prepare/pallas_call | solution.py:284
  27.7 2.0 %all-to-all-done = f32[16,32,128]{2,1,0:T(8,128)S(1)} async-done(((f32[16,32,128]{2,1,0:T(8,128)}), f32[16,32,128]{2,1,0:T(8,128)S(1)}, u32[]{:S(2)}, u32[]{:S(2)}) %all-to-all-start) | async-done | bytes 262176 | tf_op jit(solution)/shard_map/all_to_all | solution.py:307
  29.6 1.2 %phase1.1 = f32[512,128]{1,0:T(8,128)S(1)} custom-call(f32[16,2,16,128]{3,2,1,0:T(8,128)S(1)} %bitcast.15, bf16[256,128]{1,0:T(8,128)(2,1)S(1)} %get-tuple-element.24.l01h, bf16[256,128]{1,0:T(8,128)(2,1)S(1)} %get-tuple-element.25.l01l, bf16[256,128]{1,0:T(8,128)(2,1)S(1)} %get-tuple-element.26.m0h, bf16[256,128]{1,0:T(8,128)(2,1)S(1)} %get-tuple-element.27.m0l, ...), custom_call_target="tpu_custom_call" | custom-call | flops 209715200 | bytes 4194304 | tf_op jit(solution)/shard_map/phase1/pallas_call | solution.py:284
  30.9 31.0 %all_to_all.20 = f32[64,8,128]{2,1,0:T(8,128)S(1)} all-to-all(f32[64,8,128]{2,1,0:T(8,128)S(1)} %bitcast.16), channel_id=1, replica_groups=mesh['far'=16,'near'=64] {'near'}, dimensions={0} | all-to-all | bytes 524288 | tf_op jit(solution)/shard_map/all_to_all | solution.py:310
  61.9 0.8 phase2.1
  62.8 12.0 %all_to_all.21 = f32[16,32,128]{2,1,0:T(8,128)S(1)} all-to-all(f32[16,32,128]{2,1,0:T(8,128)S(1)} %bitcast.20), channel_id=1, replica_groups=mesh['far'=16,'near'=64] {'far'}, dimensions={0} | all-to-all | bytes 524288 | tf_op jit(solution)/shard_map/all_to_all | solution.py:307
  74.8 1.1 %phase3.1 = f32[512,128]{1,0:T(8,128)S(1)} custom-call(f32[16,2,2,8,128]{4,3,2,1,0:T(8,128)S(1)} %bitcast.17, bf16[512,256]{1,0:T(8,128)(2,1)S(1)} %get-tuple-element.36.w4h, bf16[512,256]{1,0:T(8,128)(2,1)S(1)} %get-tuple-element.37.w4l, bf16[512,256]{1,0:T(8,128)(2,1)S(1)} %get-tuple-element.38.w56h, bf16[512,256]{1,0:T(8,128)(2,1)S(1)} %get-tuple-element.39.w56l, ...), custom_call_target="tpu_custom_call" | custom-call | flops 209715200 | bytes 4194304 | tf_op jit(solution)/shard_map/phase3/pallas_call | solution.py:284
  75.9 22.5 %all_to_all.22 = f32[64,8,128]{2,1,0:T(8,128)S(1)} all-to-all(f32[64,8,128]{2,1,0:T(8,128)S(1)} %bitcast.18), channel_id=1, replica_groups=mesh['far'=16,'near'=64] {'near'}, dimensions={0} | all-to-all | bytes 524288 | tf_op jit(solution)/shard_map/all_to_all | solution.py:310
  98.4 1.1 %phase4.1 = (f32[256,128]{1,0:T(8,128)}, f32[256,128]{1,0:T(8,128)}) custom-call(f32[512,128]{1,0:T(8,128)S(1)} %bitcast.14, bf16[512,256]{1,0:T(8,128)(2,1)S(1)} %get-tuple-element.42.w7h, bf16[512,256]{1,0:T(8,128)(2,1)S(1)} %get-tuple-element.43.w7l), custom_call_target="tpu_custom_call" | custom-call | flops 209715200 | bytes 4194304 | tf_op jit(solution)/shard_map/phase4/pallas_call | solution.py:284
Async XLA Ops:
  2.2 27.4 %all-to-all-start = ((f32[16,32,128]{2,1,0:T(8,128)}), f32[16,32,128]{2,1,0:T(8,128)S(1)}, u32[]{:S(2)}, u32[]{:S(2)}) async-start(f32[16,32,128]{2,1,0:T(8,128)} %bitcast.2), calls=%async_computation | async-start | bytes 524288 | tf_op jit(solution)/shard_map/all_to_all | solution.py:307

commit v9 on v7

--- a/solution.py
+++ b/solution.py
@@ -19,7 +19,10 @@
 
 def mm(a, b, dims=NN):
     dot = functools.partial(lax.dot_general, dimension_numbers=dims, preferred_element_type=F32)
-    return dot(a[0], b[0]) + (dot(a[0], b[1]) + dot(a[1], b[0]))
+    k = 0 if dims is NT else 1
+    r = dot(a[0], cat(b, k))
+    n = r.shape[1] // 2
+    return r[:, :n] + (r[:, n:] + dot(a[1], b[0]))
 
 
 def mm_rows(a, b, dims=NN, step=128):

time: 99.9 us -> 99.7 us (level)
  no operation moved by 1% of the time
where the time goes in v9:
time: 99.7 us; the launch traced here: 99.3 us
  blocking collectives  65.4 us (66%)
  starting transfers between devices  18.5 us (19%)
  Pallas kernels  12.7 us (13%)
  waiting for transfers between devices  2.17 us (2%)
    all_to_all x2, blocking collectives, near(): x = lax.all_to_all(x.reshape(64, 8, 128), 'near', 0, 0, tiled=True)  53.5 us
    all_to_all x1, starting transfers between devices, far(): return lax.all_to_all(x.reshape(16, 32, 128), 'far', 0, 0, tiled=True)  18.5 us
    pallas_call x6, Pallas kernels, call(): pl.pallas_call(kernel, out_shape=out_shape, compiler_params=PARAMS, cost_...  12.7 us
    all_to_all x1, blocking collectives, far(): return lax.all_to_all(x.reshape(16, 32, 128), 'far', 0, 0, tiled=True)  11.8 us
    all_to_all x1, waiting for transfers between devices, far(): return lax.all_to_all(x.reshape(16, 32, 128), 'far', 0, 0, tiled=True)  2.17 us
  transfers between devices with their start and end apart: 1, of which 1 were waited for; matrix products, arithmetic and copies ran while one was open for 0% of the time, Pallas kernels for 7%

profile of v9, /device:TPU:1, one launch (start us, length us, event | category | flops | bytes accessed | tf_op | source)
XLA Modules:
  0.0 99.3 jit_solution(10623285057230317366)
XLA Ops:
  0.6 1.7 %phase0.1 = f32[16,2,16,128]{3,2,1,0:T(8,128)} custom-call(f32[16,16,128]{2,1,0:T(8,128)} %bitcast.21, f32[16,16,128]{2,1,0:T(8,128)} %bitcast.22), custom_call_target="tpu_custom_call" | custom-call | flops 1048576 | bytes 4194304 | tf_op jit(solution)/shard_map/phase0/pallas_call | solution.py:279
  2.3 18.5 %all-to-all-start = ((f32[16,32,128]{2,1,0:T(8,128)}), f32[16,32,128]{2,1,0:T(8,128)S(1)}, u32[]{:S(2)}, u32[]{:S(2)}) async-start(f32[16,32,128]{2,1,0:T(8,128)} %bitcast.2), calls=%async_computation | async-start | bytes 524288 | tf_op jit(solution)/shard_map/all_to_all | solution.py:302
  20.8 6.8 %prepare.1 = (bf16[256,128]{1,0:T(8,128)(2,1)S(1)}, bf16[256,128]{1,0:T(8,128)(2,1)S(1)}, bf16[256,128]{1,0:T(8,128)(2,1)S(1)}, bf16[256,128]{1,0:T(8,128)(2,1)S...) custom-call(f32[3072,128]{1,0:T(8,128)} %bitcast.23, ...), custom_call_target="tpu_custom_call" | custom-call | flops 2516582400 | bytes 4194304 | tf_op jit(solution)/shard_map/prepare/pallas_call | solution.py:279
  27.6 2.2 %all-to-all-done = f32[16,32,128]{2,1,0:T(8,128)S(1)} async-done(((f32[16,32,128]{2,1,0:T(8,128)}), f32[16,32,128]{2,1,0:T(8,128)S(1)}, u32[]{:S(2)}, u32[]{:S(2)}) %all-to-all-start) | async-done | bytes 262176 | tf_op jit(solution)/shard_map/all_to_all | solution.py:302
  29.7 1.2 %phase1.1 = f32[512,128]{1,0:T(8,128)S(1)} custom-call(f32[16,2,16,128]{3,2,1,0:T(8,128)S(1)} %bitcast.15, bf16[256,128]{1,0:T(8,128)(2,1)S(1)} %get-tuple-element.24.l01h, bf16[256,128]{1,0:T(8,128)(2,1)S(1)} %get-tuple-element.25.l01l, bf16[256,128]{1,0:T(8,128)(2,1)S(1)} %get-tuple-element.26.m0h, bf16[256,128]{1,0:T(8,128)(2,1)S(1)} %get-tuple-element.27.m0l, ...), custom_call_target="tpu_custom_call" | custom-call | flops 209715200 | bytes 4194304 | tf_op jit(solution)/shard_map/phase1/pallas_call | solution.py:279
  31.0 31.0 %all_to_all.20 = f32[64,8,128]{2,1,0:T(8,128)S(1)} all-to-all(f32[64,8,128]{2,1,0:T(8,128)S(1)} %bitcast.16), channel_id=1, replica_groups=mesh['far'=16,'near'=64] {'near'}, dimensions={0} | all-to-all | bytes 524288 | tf_op jit(solution)/shard_map/all_to_all | solution.py:305
  62.0 0.8 phase2.1
  62.9 11.8 %all_to_all.21 = f32[16,32,128]{2,1,0:T(8,128)S(1)} all-to-all(f32[16,32,128]{2,1,0:T(8,128)S(1)} %bitcast.20), channel_id=1, replica_groups=mesh['far'=16,'near'=64] {'far'}, dimensions={0} | all-to-all | bytes 524288 | tf_op jit(solution)/shard_map/all_to_all | solution.py:302
  74.7 1.1 %phase3.1 = f32[512,128]{1,0:T(8,128)S(1)} custom-call(f32[16,2,2,8,128]{4,3,2,1,0:T(8,128)S(1)} %bitcast.17, bf16[512,256]{1,0:T(8,128)(2,1)S(1)} %get-tuple-element.36.w4h, bf16[512,256]{1,0:T(8,128)(2,1)S(1)} %get-tuple-element.37.w4l, bf16[512,256]{1,0:T(8,128)(2,1)S(1)} %get-tuple-element.38.w56h, bf16[512,256]{1,0:T(8,128)(2,1)S(1)} %get-tuple-element.39.w56l, ...), custom_call_target="tpu_custom_call" | custom-call | flops 209715200 | bytes 4194304 | tf_op jit(solution)/shard_map/phase3/pallas_call | solution.py:279
  75.8 22.5 %all_to_all.22 = f32[64,8,128]{2,1,0:T(8,128)S(1)} all-to-all(f32[64,8,128]{2,1,0:T(8,128)S(1)} %bitcast.18), channel_id=1, replica_groups=mesh['far'=16,'near'=64] {'near'}, dimensions={0} | all-to-all | bytes 524288 | tf_op jit(solution)/shard_map/all_to_all | solution.py:305
  98.3 1.1 %phase4.1 = (f32[256,128]{1,0:T(8,128)}, f32[256,128]{1,0:T(8,128)}) custom-call(f32[512,128]{1,0:T(8,128)S(1)} %bitcast.14, bf16[512,256]{1,0:T(8,128)(2,1)S(1)} %get-tuple-element.42.w7h, bf16[512,256]{1,0:T(8,128)(2,1)S(1)} %get-tuple-element.43.w7l), custom_call_target="tpu_custom_call" | custom-call | flops 209715200 | bytes 4194304 | tf_op jit(solution)/shard_map/phase4/pallas_call | solution.py:279
Async XLA Ops:
  2.3 27.4 %all-to-all-start = ((f32[16,32,128]{2,1,0:T(8,128)}), f32[16,32,128]{2,1,0:T(8,128)S(1)}, u32[]{:S(2)}, u32[]{:S(2)}) async-start(f32[16,32,128]{2,1,0:T(8,128)} %bitcast.2), calls=%async_computation | async-start | bytes 524288 | tf_op jit(solution)/shard_map/all_to_all | solution.py:302
